TPU v7x, 32 devices: a whole 2x2x4 slice. The times are simulated.
32 devices in a mesh: inst: 4 (over z), scen: 8 (over y, x, core).
Axes of the slice: x: 2, y: 2, z: 4, core: 2. Of those that a mesh axis runs over, the one named last changes fastest.
Arguments:
- factor_returns: bfloat16 [8192, 64], P('scen'), may hold values from -0.8984375 to 0.8984375
- betas: bfloat16 [4000, 128], P('inst'), may hold values from -0.75 to 0.75
- base_state: bfloat16 [2, 4000], P(None, 'inst'), may hold values from 0.19921875 to 1
- underlying_slot: int32 [4000], replicated, may hold values from 0 to 3999, as said below
- chain_map: int32 [4096], replicated, may hold values from 0 to 3999, as said below
- strike_index: int32 [4096], P('inst'), may hold values from -8 to 8
- expiry: float32 [4096], P('inst'), may hold values from 0.05 to 2
- positions: int32 [1024, 4096], P(None, 'inst'), may hold values from -8 to 8
Outputs:
- losses: float32 [1024, 8192], P('inst', 'scen')
- margin: float32 [1024], P('inst')
Inputs may be any that keep to these rules, and one draw needn't show every extreme that they name: A permutation: underlying u's loadings and base state stand in row underlying_slot[u]; rows k * 1000 to (k + 1) * 1000 - 1 form owner block k. `chain_map`: the options of each block of 1024 consecutive options name, among the underlyings whose slots lie in any one owner block of 1000 slots, at most 48 distinct underlyings; in every block of options exactly 48 for some owner block. Options of one underlying stand next to each other within a block.
All inputs are finite; a program needn't handle non-finite values.
Results may differ from a plain program's by a relative error of at most 0.02.
Values may be sent and summed in bfloat16 or wider, within the bound.
A program may use at most 64 MiB of HBM per device.

v0:
```python
import jax
import jax.numpy as jnp
from jax import lax
from jax.sharding import PartitionSpec as P

F = 64
CAP = 48


strike_step = 0.05
contract_size = 0.03125


def normal_cdf(points):
    return 0.5 * lax.erfc(-points * 0.7071067811865476)


def option_value(forward, volatility, strike_level, expiry, call_flags):
    spread = volatility * jnp.sqrt(expiry)
    upper_arg = (jnp.log(forward / strike_level) + 0.5 * spread * spread) / spread
    lower_arg = upper_arg - spread
    call_value = forward * normal_cdf(upper_arg) - strike_level * normal_cdf(lower_arg)
    put_value = strike_level * normal_cdf(-lower_arg) - forward * normal_cdf(-upper_arg)
    return jnp.where(call_flags, call_value, put_value)


def scenario_rows(loadings, base_rows, factor_returns):
    shock_price = jnp.einsum(
        "...f,sf->...s", loadings[..., :F], factor_returns, preferred_element_type=jnp.float32
    )
    shock_vol = jnp.einsum(
        "...f,sf->...s", loadings[..., F:], factor_returns, preferred_element_type=jnp.float32
    )
    base_values = base_rows.astype(jnp.float32)
    scen_forward = (base_values[..., 0:1] * jnp.exp(shock_price)).astype(jnp.bfloat16)
    scen_vol = (base_values[..., 1:2] * jnp.exp(shock_vol)).astype(jnp.bfloat16)
    return jnp.concatenate([scen_forward, scen_vol], axis=-1)


def body(
    factor_returns, betas, base_state, underlying_slot, chain_map, strike_index, expiry, positions
):
    n_inst = lax.axis_size("inst")
    myself = lax.axis_index("inst")
    owner_rows = betas.shape[0]
    option_rows = strike_index.shape[0]
    scen_cols = factor_returns.shape[0]
    all_slots = underlying_slot[chain_map]
    holder = jnp.arange(chain_map.shape[0], dtype=jnp.int32) // option_rows
    needed = jnp.zeros((underlying_slot.shape[0], n_inst), jnp.int32).at[all_slots, holder].max(1)
    needed = needed.reshape(n_inst, owner_rows, n_inst)
    rank_table = jnp.cumsum(needed, axis=1) - 1
    own_need = lax.dynamic_index_in_dim(needed, myself, 0, keepdims=False)
    own_rank = lax.dynamic_index_in_dim(rank_table, myself, 0, keepdims=False)
    slot_place = jnp.arange(CAP, dtype=jnp.int32)
    select = (
        (own_rank.T[:, None, :] == slot_place[None, :, None]) & (own_need.T[:, None, :] > 0)
    ).astype(jnp.bfloat16)
    base_rows = base_state.T
    send_base = jnp.einsum(
        "dcr,rk->dck", select, base_rows, preferred_element_type=jnp.float32
    ).astype(jnp.bfloat16)
    owner_table = scenario_rows(betas, base_rows, factor_returns)
    send_rows = jnp.einsum(
        "dcr,rk->dck", select, owner_table, preferred_element_type=jnp.float32
    ).astype(jnp.bfloat16)
    got_rows, got_base = (
        lax.all_to_all(send_rows, "inst", split_axis=0, concat_axis=0, tiled=True),
        lax.all_to_all(send_base, "inst", split_axis=0, concat_axis=0, tiled=True),
    )
    my_slots = lax.dynamic_slice_in_dim(all_slots, myself * option_rows, option_rows)
    my_rank = lax.dynamic_index_in_dim(rank_table, myself, 2, keepdims=False).reshape(-1)
    source = my_slots // owner_rows
    lookup = source * CAP + my_rank[my_slots]
    option_table = jnp.take(got_rows.reshape(n_inst * CAP, 2 * scen_cols), lookup, axis=0)
    option_base = jnp.take(got_base.reshape(n_inst * CAP, 2), lookup, axis=0).astype(jnp.float32)
    forward = option_table[:, :scen_cols].astype(jnp.float32)
    volatility = option_table[:, scen_cols:].astype(jnp.float32)
    forward_zero = option_base[:, 0:1]
    vol_zero = option_base[:, 1:2]
    strike_level = forward_zero * jnp.exp(strike_step * strike_index.astype(jnp.float32))[:, None]
    call_flags = (strike_index >= 0)[:, None]
    option_expiry = expiry[:, None]
    scen_value = option_value(forward, volatility, strike_level, option_expiry, call_flags)
    base_value = option_value(forward_zero, vol_zero, strike_level, option_expiry, call_flags)
    profit = (scen_value - base_value).astype(jnp.bfloat16)
    held_counts = positions.astype(jnp.bfloat16)
    losses = lax.psum_scatter(
        (contract_size * jnp.dot(held_counts, profit, preferred_element_type=jnp.float32)).astype(
            jnp.bfloat16
        ),
        "inst",
        scatter_dimension=0,
        tiled=True,
    ).astype(jnp.float32)
    margin = lax.pmax(jnp.max(losses, axis=1), "scen")
    return (losses, margin)


def solution(mesh):
    return jax.shard_map(
        body,
        mesh=mesh,
        in_specs=(
            P("scen", None),
            P("inst", None),
            P(None, "inst"),
            P(),
            P(),
            P("inst"),
            P("inst"),
            P(None, "inst"),
        ),
        out_specs=(P("inst", "scen"), P("inst")),
        check_vma=False,
    )
```

profile of v0, /device:TPU:0, one launch (start us, length us, event | category | flops | bytes accessed | tf_op | source)
XLA Modules:
  0.0 221.9 jit_solution(8240182913302086173)
XLA Ops:
  7.2 0.0 copy-start
  7.2 0.0 copy-start.1
  7.2 0.8 fusion.101
  8.0 0.0 copy-done.1
  8.0 0.0 copy-start.5
  8.0 0.0 copy-start.3
  8.0 0.0 copy-start.2
  8.0 0.0 copy-start.4
  8.0 0.0 copy-start.8
  8.0 23.0 %gather_fusion = s32[4096]{0:T(1024)S(1)} fusion(s32[4000]{0:T(1024)S(1)} %copy-done.1, s32[4096]{0:T(1024)S(1)} %fusion.101), kind=kCustom, calls=%fused_computation | custom fusion | bytes 49152 | tf_op jit(solution)/shard_map/gather | solution.py:48
  31.1 0.0 copy-done.6
  31.1 0.1 and_reduce_fusion
  31.2 0.0 copy-done.5
  31.3 0.1 multiply_reduce_fusion
  31.4 27.2 %scatter_custom_fusion = s32[16000]{0:T(1024)S(1)} fusion(s32[4096]{0:T(1024)S(1)} %broadcast_select_fusion.1, s32[4096]{0:T(1024)S(1)} %broadcast.376, s32[]{:T(128)} %constant.48.clone.1), kind=kCustom, calls=%fused_computation.151 | custom fusion | flops 4096 | bytes 64004
  58.6 0.1 reshape.104
  58.8 0.1 reshape.96
  59.0 4.5 %reduce-window.6 = s32[4,4,8,128]{3,2,1,0:T(8,128)S(1)} reduce-window(s32[4,4,8,128]{3,2,1,0:T(8,128)S(1)} %copy.25, s32[]{:T(128)} %constant.48.clone.1), window={size=1x1x1x128 pad=0_0x0_0x0_0x127_0}, to_apply=%region_1.2 | reduce-window | flops 2080768 | bytes 131076 | tf_op jit(solution)/shard_map/reduce-window
  63.5 0.4 slice_reduce_fusion
  64.0 0.7 reduce-window.9
  64.7 0.1 broadcast_add_fusion
  64.9 0.0 copy-done.3
  64.9 0.9 convolution_convert_fusion
  65.8 6.3 %all-to-all-start.1 = ((bf16[4,48,2]{1,2,0:T(2,128)(2,1)}), bf16[4,48,2]{1,2,0:T(2,128)(2,1)S(1)}, u32[]{:S(2)}, u32[]{:S(2)}) async-start(bf16[4,48,2]{1,2,0:T(2,128)(2,1)} %convolution_convert_fusion), calls=%async_computation.1 | async-start | bytes 4096 | tf_op jit(solution)/shard_map/all_to_all | solution.py:69
  72.1 0.0 copy-done.2
  72.1 0.0 copy-done.4
  72.2 0.8 multiply_convert_fusion.1
  73.0 0.7 multiply_convert_fusion.2
  73.7 2.1 fusion.46
  75.8 0.1 dynamic-slice_reduce_fusion
  75.8 0.1 reshape.99
  75.9 1.6 all-to-all-done.1
  77.5 3.5 %all-to-all-start = ((bf16[4,48,2048]{2,1,0:T(8,128)(2,1)}), bf16[4,48,2048]{2,1,0:T(8,128)(2,1)S(1)}, u32[]{:S(2)}, u32[]{:S(2)}) async-start(bf16[4,48,2048]{2,1,0:T(8,128)(2,1)} %fusion.46), calls=%async_computation | async-start | bytes 1572864 | tf_op jit(solution)/shard_map/all_to_all | solution.py:68
  81.1 6.2 %gather_fusion.1 = s32[1024]{0:T(1024)S(1)} fusion(s32[4000]{0:T(1024)S(1)} %reshape.99, s32[1024]{0:T(1024)S(1)} %fusion.111), kind=kCustom, calls=%fused_computation.1 | custom fusion | bytes 12288 | tf_op jit(solution)/shard_map/gather | solution.py:74
  87.3 0.1 copy.30
  87.4 3.2 %gather_fusion.3 = bf16[1024,2]{1,0:T(8,128)(2,1)S(1)} fusion(bf16[192,2]{1,0:T(8,128)(2,1)S(1)} %bitcast.43, s32[1024]{0:T(1024)S(1)} %broadcast_clamp_fusion), kind=kCustom, calls=%fused_computation.3 | custom fusion | bytes 12288 | tf_op jit(solution)/shard_map/jit(_take)/gather | solution.py:76
  90.6 0.1 copy.28
  90.8 0.3 reshape_select_fusion
  91.1 9.5 %all-to-all-done = bf16[4,48,2048]{2,1,0:T(8,128)(2,1)S(1)} async-done(((bf16[4,48,2048]{2,1,0:T(8,128)(2,1)}), bf16[4,48,2048]{2,1,0:T(8,128)(2,1)S(1)}, u32[]{:S(2)}, u32[]{:S(2)}) %all-to-all-start) | async-done | bytes 786464 | tf_op jit(solution)/shard_map/all_to_all | solution.py:68
  100.6 6.0 %gather_fusion.2 = bf16[1024,2048]{1,0:T(8,128)(2,1)} fusion(bf16[192,2048]{1,0:T(8,128)(2,1)S(1)} %bitcast.42, s32[1024]{0:T(1024)S(1)} %broadcast_clamp_fusion), kind=kCustom, calls=%fused_computation.2 | custom fusion | bytes 8392704 | tf_op jit(solution)/shard_map/jit(_take)/gather | solution.py:75
  106.6 2.8 %broadcast_select_fusion = bf16[1024,2048]{1,0:T(8,128)(2,1)S(1)} fusion(bf16[1024,2048]{1,0:T(8,128)(2,1)} %gather_fusion.2, pred[1024]{0:T(1024)(128)(4,1)S(1)} %get-tuple-element.12), kind=kLoop, calls=%fused_computation.82 | loop fusion | flops 2097152 | bytes 8389632 | tf_op jit(solution)/shard_map/jit(_take)/select_n | solution.py:75
  109.4 0.7 copy-done.7
  110.0 44.5 %fusion.85 = bf16[1024,1024]{0,1:T(8,128)(2,1)} fusion(s32[1024,1024]{1,0:T(8,128)S(1)} %copy-done.7, bf16[1024,2048]{1,0:T(8,128)(2,1)S(1)} %broadcast_select_fusion, f32[1024]{0:T(1024)S(1)} %bitcast.55, f32[1024]{0:T(1024)S(1)} %broadcast_multiply_fusion, f32[1024]{0:T(1024)S(1)} %sqrt.7, f32[1024]{0:T(1024)S(1)} %bitcast.52, ...), kind=kOutput, calls=%fused_computation.133 | convolution fusion | flops 2429550592 | bytes 10503168 | tf_op jit(solution)/shard_map/dot_general | solution.py:89
  154.5 0.0 reduce-scatter.2.cloned.1.call-update
  154.6 43.1 %reduce-scatter.2.cloned.1.call-done = bf16[256,1024]{0,1:T(8,128)(2,1)} async-done(((bf16[1024,1024]{0,1:T(8,128)(2,1)}), bf16[256,1024]{0,1:T(8,128)(2,1)}) %reduce-scatter.2.cloned.1.call-update) | async-done | bytes 524304 | tf_op jit(solution)/shard_map/reduce_scatter | solution.py:88
  197.7 1.2 reduce_max.14
  198.9 14.0 %pmax.7 = f32[256]{0:T(256)} all-reduce(bf16[256]{0:T(256)(128)(2,1)S(1)} %reduce_max.14), channel_id=1, replica_groups=mesh['inst'=4,'scen'=8] {'scen'}, use_global_device_ids=true, to_apply=%region_5.6 | all-reduce | flops 256 | bytes 1536 | tf_op jit(solution)/shard_map/pmax | solution.py:96
  212.9 2.2 copy.29
  (26 shorter events, 0.3 us)
Async XLA Ops:
  7.2 65.0 %copy-start = (bf16[1024,64]{0,1:T(8,128)(2,1)S(1)}, bf16[1024,64]{0,1:T(8,128)(2,1)}, u32[]{:S(2)}) copy-start(bf16[1024,64]{0,1:T(8,128)(2,1)} %param.8) | copy-start | bytes 393220
  7.2 0.8 copy-start.1
  8.0 23.2 %copy-start.6 = (s32[2]{0:T(128)S(1)}, s32[2]{0:T(128)}, u32[]{:S(2)}) copy-start(s32[2]{0:T(128)} %constant.100) | copy-start | bytes 28
  8.0 23.3 %copy-start.5 = (s32[2]{0:T(128)S(1)}, s32[2]{0:T(128)}, u32[]{:S(2)}) copy-start(s32[2]{0:T(128)} %constant.97) | copy-start | bytes 28
  8.0 56.9 %copy-start.3 = (bf16[2,1000]{1,0:T(2,128)(2,1)S(1)}, bf16[2,1000]{1,0:T(2,128)(2,1)}, u32[]{:S(2)}) copy-start(bf16[2,1000]{1,0:T(2,128)(2,1)} %param.10) | copy-start | bytes 12004
  8.0 64.1 %copy-start.2 = (s32[1024]{0:T(1024)S(1)}, s32[1024]{0:T(1024)}, u32[]{:S(2)}) copy-start(s32[1024]{0:T(1024)} %param.13) | copy-start | bytes 12292
  8.0 64.1 %copy-start.4 = (f32[1024]{0:T(1024)S(1)}, f32[1024]{0:T(1024)}, u32[]{:S(2)}) copy-start(f32[1024]{0:T(1024)} %param.14) | copy-start | bytes 12292
  8.0 64.2 %copy-start.8 = (bf16[1000,128]{1,0:T(8,128)(2,1)S(1)}, bf16[1000,128]{1,0:T(8,128)(2,1)}, u32[]{:S(2)}) copy-start(bf16[1000,128]{1,0:T(8,128)(2,1)} %param.9) | copy-start | bytes 768004
  65.8 11.7 %all-to-all-start.1 = ((bf16[4,48,2]{1,2,0:T(2,128)(2,1)}), bf16[4,48,2]{1,2,0:T(2,128)(2,1)S(1)}, u32[]{:S(2)}, u32[]{:S(2)}) async-start(bf16[4,48,2]{1,2,0:T(2,128)(2,1)} %convolution_convert_fusion), calls=%async_computation.1 | async-start | bytes 4096 | tf_op jit(solution)/shard_map/all_to_all | solution.py:69
  77.5 23.1 %all-to-all-start = ((bf16[4,48,2048]{2,1,0:T(8,128)(2,1)}), bf16[4,48,2048]{2,1,0:T(8,128)(2,1)S(1)}, u32[]{:S(2)}, u32[]{:S(2)}) async-start(bf16[4,48,2048]{2,1,0:T(8,128)(2,1)} %fusion.46), calls=%async_computation | async-start | bytes 1572864 | tf_op jit(solution)/shard_map/all_to_all | solution.py:68
  81.0 116.7 %reduce-scatter.2.cloned.1.call-start = ((), (), s32[]{:S(2)}) async-start(), calls=%async_computation.3 | async-start | bytes 2621440 | tf_op jit(solution)/shard_map/reduce_scatter | solution.py:88
  106.6 3.4 %copy-start.7 = (s32[1024,1024]{1,0:T(8,128)S(1)}, s32[1024,1024]{1,0:T(8,128)}, u32[]{:S(2)}) copy-start(s32[1024,1024]{1,0:T(8,128)} %param.15) | copy-start | bytes 12582916
Sparse Core Ops, SparseCore 0:
  154.7 42.9 reduce-scatter.1
where the time goes:
time: 222 us
  waiting for transfers between devices  54.2 us (24%)
  matrix products  49 us (22%)
  local copies, waits for them, and re-layouts  42.5 us (19%)
  other arithmetic  38.1 us (17%)
  between operations  14.4 us (6%)
  blocking collectives  14 us (6%)
  starting transfers between devices  9.87 us (4%)
    dot_general x1, matrix products, body(): jnp.dot(held_counts, profit, preferred_element_type=jnp.float32)  44.5 us
    reduce_scatter x1, waiting for transfers between devices, body(): lax.psum_scatter((contract_size * jnp.dot(held_counts, profit, preferred_...  43.1 us
    unnamed x4, other arithmetic  27.5 us
    gather x1, local copies, waits for them, and re-layouts, body(): all_slots = underlying_slot[chain_map]  23 us
    pmax x1, blocking collectives, body(): margin = lax.pmax(jnp.max(losses, axis=1), 'scen')  14 us
    all_to_all x1, waiting for transfers between devices, body(): lax.all_to_all(send_rows, 'inst', split_axis=0, concat_axis=0, tiled=True)  9.47 us
    all_to_all x1, starting transfers between devices, body(): lax.all_to_all(send_base, 'inst', split_axis=0, concat_axis=0, tiled=True)  6.32 us
    gather x1, local copies, waits for them, and re-layouts, body(): lookup = source * CAP + my_rank[my_slots]  6.15 us
  transfers between devices with their start and end apart: 3, of which 3 were waited for; matrix products, arithmetic and copies ran while one was open for 6% of the time, Pallas kernels for 0%

commit v1 on v0

v1 whole, which is shorter than its diff:
```python
import functools
import jax
import jax.numpy as jnp
from jax import lax
from jax.experimental import pallas as pl
from jax.experimental.pallas import tpu as pltpu
from jax.sharding import PartitionSpec as P

F = 64
CAP = 48
strike_step = 0.05
contract_size = 0.03125
ERF_Q = (1.1283797055307927, 0.10276548081347335, -0.0001843820436491351, -0.0006257211496349986, 8.971323300994763e-05, -5.9858035855426975e-06, 1.5896701753059672e-07)
SQRT_HALF = 0.7071067811865476


def erf_points(points):
    square = jnp.minimum(points * points, 16.0)
    poly = ERF_Q[-1]
    for coef in ERF_Q[-2::-1]:
        poly = poly * square + coef
    return jnp.tanh(points * poly)


def split_three(values):
    high = values.astype(jnp.bfloat16)
    rest = values - high.astype(jnp.float32)
    middle = rest.astype(jnp.bfloat16)
    low = (rest - middle.astype(jnp.float32)).astype(jnp.bfloat16)
    return jnp.concatenate([high, middle, low], axis=0)


def index_plan(underlying_slot, chain_map, n_inst, myself, owner_rows, option_rows):
    f32 = jnp.float32
    count = underlying_slot.shape[0]
    high_count = -(-count // 128)
    table = jnp.pad(underlying_slot, (0, high_count * 128 - count)).reshape(high_count, 128)
    tables = jnp.concatenate([table // 64, table % 64], axis=1).astype(jnp.bfloat16)
    high = (chain_map // 128)[:, None] == jnp.arange(high_count, dtype=jnp.int32)[None, :]
    rows = jnp.dot(high.astype(jnp.bfloat16), tables, preferred_element_type=f32)
    rows = rows[:, :128] * 64.0 + rows[:, 128:]
    low = (chain_map % 128)[:, None] == jnp.arange(128, dtype=jnp.int32)[None, :]
    slots = jnp.sum(jnp.where(low, rows, 0.0), axis=1).astype(jnp.int32)
    slots = slots.reshape(n_inst, option_rows)
    blocks = chain_map.reshape(n_inst, option_rows)
    first = jnp.concatenate(
        [jnp.ones((n_inst, 1), bool), blocks[:, 1:] != blocks[:, :-1]], axis=1
    )
    owner = slots // owner_rows
    owners = jnp.arange(n_inst, dtype=jnp.int32)
    fresh = first[:, None, :] & (owner[:, None, :] == owners[None, :, None])
    parts = option_rows // 128
    upper = (jnp.arange(128)[:, None] <= jnp.arange(128)[None, :]).astype(jnp.bfloat16)
    inner = jnp.dot(
        fresh.astype(jnp.bfloat16).reshape(n_inst * n_inst * parts, 128),
        upper,
        preferred_element_type=f32,
    ).reshape(n_inst, n_inst, parts, 128)
    totals = inner[..., -1]
    before = jnp.arange(parts)[:, None] < jnp.arange(parts)[None, :]
    offsets = jnp.sum(jnp.where(before, totals[..., :, None], 0.0), axis=2)
    running = (inner + offsets[..., None]).reshape(n_inst, n_inst, option_rows)
    ranks = running.astype(jnp.int32) - 1
    own_rank = lax.dynamic_index_in_dim(ranks, myself, 1, keepdims=False)
    own_fresh = lax.dynamic_index_in_dim(fresh, myself, 1, keepdims=False)
    place = jnp.arange(CAP, dtype=jnp.int32)
    hit = (own_rank[:, None, :] == place[None, :, None]) & own_fresh[:, None, :]
    local = slots - myself * owner_rows + 1
    send_row = jnp.sum(jnp.where(hit, local[:, None, :], 0), axis=2) - 1
    my_rank = lax.dynamic_index_in_dim(ranks, myself, 0, keepdims=False)
    my_owner = lax.dynamic_index_in_dim(owner, myself, 0, keepdims=False)
    rank_here = jnp.sum(jnp.where(my_owner[None, :] == owners[:, None], my_rank, 0), axis=0)
    return send_row, my_owner * CAP + rank_here


def price_kernel(fr_ref, loads_ref, base_ref, expand_ref, params_ref, pos_ref, out_ref, held, pnl, lf_sc, rv_sc, f_sc, v_sc):
    options = expand_ref.shape[0]
    f32 = jnp.float32

    @pl.when(pl.program_id(0) == 0)
    def _():
        held[...] = (pos_ref[...].astype(f32) * contract_size).astype(jnp.bfloat16)

    loads = loads_ref[...]
    dims = (((1,), (1,)), ((), ()))
    shock_price = lax.dot_general(loads[:, :F], fr_ref[...], dims, preferred_element_type=f32)
    shock_vol = lax.dot_general(loads[:, F:], fr_ref[...], dims, preferred_element_type=f32)
    base = base_ref[...].astype(f32)
    forward = (base[:, 0:1] * jnp.exp(shock_price)).astype(jnp.bfloat16)
    vol = (base[:, 1:2] * jnp.exp(shock_vol)).astype(jnp.bfloat16)
    forward_wide = forward.astype(f32)
    vol_wide = vol.astype(f32)
    live = forward_wide > 0.0
    f_sc[...] = forward
    v_sc[...] = vol
    lf_sc[...] = split_three(jnp.log(jnp.where(live, forward_wide, 1.0)))
    rv_sc[...] = split_three(1.0 / jnp.where(live, vol_wide, 1.0))

    tile = 128

    def step(index, carry):
        rows = pl.ds(pl.multiple_of(index * tile, tile), tile)
        pick = expand_ref[rows, :]
        pick3 = jnp.concatenate([pick, pick, pick], axis=1)
        fwd = jnp.dot(pick, f_sc[...], preferred_element_type=f32)
        sig = jnp.dot(pick, v_sc[...], preferred_element_type=f32)
        log_f = jnp.dot(pick3, lf_sc[...], preferred_element_type=f32)
        inv_v = jnp.dot(pick3, rv_sc[...], preferred_element_type=f32)
        par = params_ref[rows, :]
        log_k, c1, c2 = par[:, 0:1], par[:, 1:2], par[:, 2:3]
        half_k, half_phi, v0 = par[:, 3:4], par[:, 4:5], par[:, 5:6]
        ratio = (log_f - log_k) * (inv_v * c1)
        half = sig * c2
        e1 = erf_points(ratio + half)
        e2 = erf_points(ratio - half)
        flat = par[:, 6:7]
        value = fwd * (half_phi + 0.5 * e1) - half_k * e2 - flat
        pnl[rows, :] = value.astype(jnp.bfloat16)
        return carry

    lax.fori_loop(0, options // tile, step, 0)
    out_ref[...] = jnp.dot(held[...], pnl[...], preferred_element_type=f32).astype(out_ref.dtype)


def body(
    factor_returns, betas, base_state, underlying_slot, chain_map, strike_index, expiry, positions
):
    n_inst = lax.axis_size("inst")
    myself = lax.axis_index("inst")
    owner_rows = betas.shape[0]
    option_rows = strike_index.shape[0]
    scen_cols = factor_returns.shape[0]
    accounts = positions.shape[0]
    f32 = jnp.float32
    send_row, lookup = index_plan(
        underlying_slot, chain_map, n_inst, myself, owner_rows, option_rows
    )
    select = (
        send_row.reshape(-1)[:, None] == jnp.arange(owner_rows, dtype=jnp.int32)[None, :]
    ).astype(jnp.bfloat16)
    send_loads = jnp.dot(select, betas, preferred_element_type=f32).astype(jnp.bfloat16)
    send_base = lax.dot_general(
        select, base_state, (((1,), (1,)), ((), ())), preferred_element_type=f32
    ).astype(jnp.bfloat16)
    send = jnp.concatenate([send_loads, jnp.pad(send_base, ((0, 0), (0, 126)))], axis=1)
    got = lax.all_to_all(
        send.reshape(n_inst, CAP, 256), "inst", split_axis=0, concat_axis=0, tiled=True
    ).reshape(n_inst * CAP, 256)
    loads = got[:, :128]
    base = got[:, 128:130]
    places = n_inst * CAP
    expand = lookup[:, None] == jnp.arange(places, dtype=jnp.int32)[None, :]
    expand = expand.astype(jnp.bfloat16)
    option_base = lax.dot_general(
        base, expand, (((0,), (1,)), ((), ())), preferred_element_type=f32
    )
    forward_zero, vol_zero = option_base[0], option_base[1]
    log_step = strike_step * strike_index.astype(f32)
    strike = forward_zero * jnp.exp(log_step)
    log_k = jnp.log(strike)
    root = jnp.sqrt(expiry)
    c1 = SQRT_HALF / root
    c2 = (0.5 * SQRT_HALF) * root
    half_phi = jnp.where(strike_index >= 0, 0.5, -0.5)
    ratio = -log_step / vol_zero * c1
    half = vol_zero * c2
    e1 = lax.erf(ratio + half)
    e2 = lax.erf(ratio - half)
    half_k = 0.5 * strike
    v0 = forward_zero * (half_phi + 0.5 * e1) - strike * (half_phi + 0.5 * e2)
    flat = v0 + half_phi * strike
    zero = jnp.zeros_like(v0)
    params = jnp.stack([log_k, c1, c2, half_k, half_phi, v0, flat, zero], axis=1)
    chunk = min(256, scen_cols)
    whole = pl.BlockSpec(memory_space=pltpu.VMEM)
    partial = pl.pallas_call(
        price_kernel,
        grid=(scen_cols // chunk,),
        out_shape=jax.ShapeDtypeStruct((accounts, scen_cols), jnp.bfloat16),
        in_specs=[pl.BlockSpec((chunk, F), lambda i: (i, 0)), whole, whole, whole, whole, whole],
        out_specs=pl.BlockSpec((accounts, chunk), lambda i: (0, i)),
        scratch_shapes=[
            pltpu.VMEM((accounts, option_rows), jnp.bfloat16),
            pltpu.VMEM((option_rows, chunk), jnp.bfloat16),
            pltpu.VMEM((3 * places, chunk), jnp.bfloat16),
            pltpu.VMEM((3 * places, chunk), jnp.bfloat16),
            pltpu.VMEM((places, chunk), jnp.bfloat16),
            pltpu.VMEM((places, chunk), jnp.bfloat16),
        ],
        compiler_params=pltpu.CompilerParams(vmem_limit_bytes=40 * 1024 * 1024),
    )(factor_returns, loads, base, expand, params, positions)
    losses = lax.psum_scatter(partial, "inst", scatter_dimension=0, tiled=True).astype(f32)
    margin = lax.pmax(jnp.max(losses, axis=1), "scen")
    return (losses, margin)


def solution(mesh):
    return jax.shard_map(
        body,
        mesh=mesh,
        in_specs=(
            P("scen", None),
            P("inst", None),
            P(None, "inst"),
            P(),
            P(),
            P("inst"),
            P("inst"),
            P(None, "inst"),
        ),
        out_specs=(P("inst", "scen"), P("inst")),
        check_vma=False,
    )
```

time: 222 us -> 116 us (0.52)
  matrix products: 49 us -> 1.95 us
  local copies, waits for them, and re-layouts: 42.5 us -> 4.6 us
  other arithmetic: 38.1 us -> 5.17 us
  Pallas kernels: 0 us -> 21.3 us
  waiting for transfers between devices: 54.2 us -> 48.1 us
  starting transfers between devices: 9.87 us -> 6.32 us
    dot_general x5, matrix products: 49 us -> 1.95 us  [the longest x1 0.74 us: index_plan(): jnp.dot(high.astype(jnp.bfloat16), tables, preferred_element_type=f32)]
    gather x5 -> x0, local copies, waits for them, and re-layouts: 38.5 us -> none  [the longest x1 23 us: body(): all_slots = underlying_slot[chain_map]]
    unnamed x4 -> x0, other arithmetic: 27.5 us -> none
    pallas_call x0 -> x1, Pallas kernels: none -> 21.3 us  [body(): pl.pallas_call(price_kernel, grid=(scen_cols // chunk,), out_shape=jax.Sh...]
    all_to_all x2 -> x1, waiting for transfers between devices: 11 us -> 5.38 us  [body(): lax.all_to_all(send.reshape(n_inst, CAP, 256), 'inst', split_axis=0, conc...]
    another operation x3 -> x1, other arithmetic: 5.33 us -> 0.74 us
    all_to_all x2 -> x1, starting transfers between devices: 9.86 us -> 6.32 us  [body(): lax.all_to_all(send.reshape(n_inst, CAP, 256), 'inst', split_axis=0, conc...]
    select_n x3, other arithmetic: 3.13 us -> 0.81 us  [the longest x1 0.78 us: index_plan(): chain_map % 128]
  transfers between devices with their start and end apart: 3 -> 2, of which waited for: 3 -> 2; matrix products, arithmetic and copies ran while one was open for 6% -> 0% of each run, Pallas kernels for 0% -> 0%
where the time goes in v1:
time: 116 us
  waiting for transfers between devices  48.1 us (41%)
  Pallas kernels  21.3 us (18%)
  between operations  14.3 us (12%)
  blocking collectives  14 us (12%)
  starting transfers between devices  6.32 us (5%)
  other arithmetic  5.17 us (4%)
  local copies, waits for them, and re-layouts  4.6 us (4%)
  matrix products  1.95 us (2%)
    reduce_scatter x1, waiting for transfers between devices, body(): lax.psum_scatter(partial, 'inst', scatter_dimension=0, tiled=True)  42.7 us
    pallas_call x1, Pallas kernels, body(): pl.pallas_call(price_kernel, grid=(scen_cols // chunk,), out_shape=jax.Sh...  21.3 us
    pmax x1, blocking collectives, body(): margin = lax.pmax(jnp.max(losses, axis=1), 'scen')  14 us
    all_to_all x1, starting transfers between devices, body(): lax.all_to_all(send.reshape(n_inst, CAP, 256), 'inst', split_axis=0, conc...  6.32 us
    all_to_all x1, waiting for transfers between devices, body(): lax.all_to_all(send.reshape(n_inst, CAP, 256), 'inst', split_axis=0, conc...  5.38 us
    unnamed x15, local copies, waits for them, and re-layouts  2.41 us
    reduce_max x1, other arithmetic, body(): margin = lax.pmax(jnp.max(losses, axis=1), 'scen')  2.35 us
  transfers between devices with their start and end apart: 2, of which 2 were waited for; matrix products, arithmetic and copies ran while one was open for 0% of the time, Pallas kernels for 0%

profile of v1, /device:TPU:0, one launch (start us, length us, event | category | flops | bytes accessed | tf_op | source)
XLA Modules:
  0.0 115.8 jit_solution(1082458822944320838)
XLA Ops:
  7.2 0.0 copy-start
  7.2 0.8 add_select_fusion.5
  8.0 0.7 reshape.99
  8.7 0.7 fusion.19
  9.4 0.7 fusion.6
  10.2 0.0 copy-start.5
  10.2 0.4 fusion.1
  10.6 0.0 copy-start.2
  10.6 0.0 copy-start.3
  10.6 0.0 copy-start.4
  10.7 0.1 slice_compare_fusion
  10.8 0.1 fusion.39
  10.9 0.1 fusion.13
  11.1 0.2 slice_reduce_fusion
  11.2 0.1 select_reduce_fusion.1
  11.4 0.1 convert_add_fusion
  11.6 0.3 select_reduce_fusion
  11.8 0.1 sub.58
  11.9 0.0 copy-done
  11.9 0.4 convolution_convert_fusion
  12.3 0.0 copy-done.5
  12.3 0.3 convolution_convert_fusion.1
  12.7 0.7 copy.32
  13.4 6.3 %all-to-all-start = ((bf16[4,48,256]{2,1,0:T(8,128)(2,1)}), bf16[4,48,256]{2,1,0:T(8,128)(2,1)S(1)}, u32[]{:S(2)}, u32[]{:S(2)}) async-start(bf16[4,48,256]{2,1,0:T(8,128)(2,1)} %bitcast.6), calls=%async_computation | async-start | bytes 196608 | tf_op jit(solution)/shard_map/all_to_all | solution.py:146
  19.7 0.0 reduce-scatter.2.cloned.1.call-start
  19.8 0.0 copy-done.2
  19.8 0.2 copy.33.fr_ref
  20.0 0.2 fusion.3.expand_ref
  20.2 5.4 %all-to-all-done = bf16[4,48,256]{2,1,0:T(8,128)(2,1)S(1)} async-done(((bf16[4,48,256]{2,1,0:T(8,128)(2,1)}), bf16[4,48,256]{2,1,0:T(8,128)(2,1)S(1)}, u32[]{:S(2)}, u32[]{:S(2)}) %all-to-all-start) | async-done | bytes 98336 | tf_op jit(solution)/shard_map/all_to_all | solution.py:146
  25.6 0.4 fusion.2
  26.0 0.0 copy-done.3
  26.0 0.0 copy-done.4
  26.0 0.1 stack.31
  26.1 0.2 copy.34.params_ref
  26.3 0.0 copy-start.1
  26.3 2.2 %copy-done.1 = s32[1024,1024]{1,0:T(8,128)S(1)} copy-done((s32[1024,1024]{1,0:T(8,128)S(1)}, s32[1024,1024]{1,0:T(8,128)}, u32[]{:S(2)}) %copy-start.1) | copy-done | bytes 4194328
  28.5 21.3 %shard_map.95 = bf16[1024,1024]{1,0:T(8,128)(2,1)} custom-call(bf16[1024,64]{1,0:T(8,128)(2,1)S(1)} %copy.33.fr_ref, bf16[192,128]{1,0:T(8,128)(2,1)S(1)} %slice.41.loads_ref, bf16[192,2]{1,0:T(8,128)(2,1)S(1)} %slice.42.base_ref, bf16[1024,192]{1,0:T(8,128)(2,1)S(1)} %fusion.3.expand_ref, f32[1024,8]{1,0:T(8,128)S(1)} %copy.34.params_ref, ...), custom_call_target="tpu_custom_call" | custom-call | tf_op jit(solution)/shard_map/pallas_call | solution.py:176
  49.8 0.0 reduce-scatter.2.cloned.1.call-update
  49.9 42.7 %reduce-scatter.2.cloned.1.call-done = bf16[256,1024]{1,0:T(8,128)(2,1)} async-done(((bf16[1024,1024]{1,0:T(8,128)(2,1)}), bf16[256,1024]{1,0:T(8,128)(2,1)}) %reduce-scatter.2.cloned.1.call-update) | async-done | bytes 524304 | tf_op jit(solution)/shard_map/reduce_scatter | solution.py:192
  92.6 2.4 %fusion.37 = (bf16[256]{0:T(256)(128)(2,1)S(1)}, f32[256,1024]{1,0:T(8,128)}) fusion(bf16[256,1024]{1,0:T(8,128)(2,1)} %reduce-scatter.2.cloned.1.call-done), kind=kLoop, calls=%fused_computation.89 | loop fusion | flops 524032 | bytes 1573376 | tf_op jit(solution)/shard_map/reduce_max | solution.py:193
  95.0 14.0 %pmax.7 = f32[256]{0:T(256)} all-reduce(bf16[256]{0:T(256)(128)(2,1)S(1)} %get-tuple-element.6), channel_id=1, replica_groups=mesh['inst'=4,'scen'=8] {'scen'}, use_global_device_ids=true, to_apply=%region_6.7 | all-reduce | flops 256 | bytes 1536 | tf_op jit(solution)/shard_map/pmax | solution.py:193
  (22 shorter events, 0.3 us)
Async XLA Ops:
  7.2 4.8 %copy-start = (bf16[1000,128]{1,0:T(8,128)(2,1)S(1)}, bf16[1000,128]{1,0:T(8,128)(2,1)}, u32[]{:S(2)}) copy-start(bf16[1000,128]{1,0:T(8,128)(2,1)} %param.9) | copy-start | bytes 768004
  10.2 2.1 %copy-start.5 = (bf16[2,1000]{1,0:T(2,128)(2,1)S(1)}, bf16[2,1000]{1,0:T(2,128)(2,1)}, u32[]{:S(2)}) copy-start(bf16[2,1000]{1,0:T(2,128)(2,1)} %param.10) | copy-start | bytes 12004
  10.6 9.2 %copy-start.2 = (bf16[1024,64]{0,1:T(8,128)(2,1)S(1)}, bf16[1024,64]{0,1:T(8,128)(2,1)}, u32[]{:S(2)}) copy-start(bf16[1024,64]{0,1:T(8,128)(2,1)} %param.8) | copy-start | bytes 393220
  10.6 15.3 %copy-start.3 = (s32[1024]{0:T(1024)S(1)}, s32[1024]{0:T(1024)}, u32[]{:S(2)}) copy-start(s32[1024]{0:T(1024)} %param.13) | copy-start | bytes 12292
  10.6 15.3 %copy-start.4 = (f32[1024]{0:T(1024)S(1)}, f32[1024]{0:T(1024)}, u32[]{:S(2)}) copy-start(f32[1024]{0:T(1024)} %param.14) | copy-start | bytes 12292
  13.4 12.2 %all-to-all-start = ((bf16[4,48,256]{2,1,0:T(8,128)(2,1)}), bf16[4,48,256]{2,1,0:T(8,128)(2,1)S(1)}, u32[]{:S(2)}, u32[]{:S(2)}) async-start(bf16[4,48,256]{2,1,0:T(8,128)(2,1)} %bitcast.6), calls=%async_computation | async-start | bytes 196608 | tf_op jit(solution)/shard_map/all_to_all | solution.py:146
  19.7 72.9 %reduce-scatter.2.cloned.1.call-start = ((), (), s32[]{:S(2)}) async-start(), calls=%async_computation.2 | async-start | bytes 2621440 | tf_op jit(solution)/shard_map/reduce_scatter | solution.py:192
  26.3 2.2 %copy-start.1 = (s32[1024,1024]{1,0:T(8,128)S(1)}, s32[1024,1024]{1,0:T(8,128)}, u32[]{:S(2)}) copy-start(s32[1024,1024]{1,0:T(8,128)} %pos_ref.1) | copy-start | bytes 12582916
Sparse Core Ops, SparseCore 0:
  50.0 42.5 reduce-scatter.1

commit v2 on v1

--- a/solution.py
+++ b/solution.py
@@ -73,13 +73,9 @@
     return send_row, my_owner * CAP + rank_here
 
 
-def price_kernel(fr_ref, loads_ref, base_ref, expand_ref, params_ref, pos_ref, out_ref, held, pnl, lf_sc, rv_sc, f_sc, v_sc):
+def price_kernel(fr_ref, loads_ref, base_ref, expand_ref, params_ref, pos_ref, out_ref, pnl, lf_sc, rv_sc, f_sc, v_sc):
     options = expand_ref.shape[0]
     f32 = jnp.float32
-
-    @pl.when(pl.program_id(0) == 0)
-    def _():
-        held[...] = (pos_ref[...].astype(f32) * contract_size).astype(jnp.bfloat16)
 
     loads = loads_ref[...]
     dims = (((1,), (1,)), ((), ()))
@@ -119,7 +115,7 @@
         return carry
 
     lax.fori_loop(0, options // tile, step, 0)
-    out_ref[...] = jnp.dot(held[...], pnl[...], preferred_element_type=f32).astype(out_ref.dtype)
+    out_ref[...] = jnp.dot(pos_ref[...], pnl[...], preferred_element_type=f32).astype(out_ref.dtype)
 
 
 def body(
@@ -172,24 +168,35 @@
     zero = jnp.zeros_like(v0)
     params = jnp.stack([log_k, c1, c2, half_k, half_phi, v0, flat, zero], axis=1)
     chunk = min(256, scen_cols)
+    pieces = min(4, scen_cols // chunk)
+    piece = scen_cols // pieces
+    held = (contract_size * positions.astype(f32)).astype(jnp.bfloat16)
     whole = pl.BlockSpec(memory_space=pltpu.VMEM)
-    partial = pl.pallas_call(
+    price = pl.pallas_call(
         price_kernel,
-        grid=(scen_cols // chunk,),
-        out_shape=jax.ShapeDtypeStruct((accounts, scen_cols), jnp.bfloat16),
+        grid=(piece // chunk,),
+        out_shape=jax.ShapeDtypeStruct((accounts, piece), jnp.bfloat16),
         in_specs=[pl.BlockSpec((chunk, F), lambda i: (i, 0)), whole, whole, whole, whole, whole],
         out_specs=pl.BlockSpec((accounts, chunk), lambda i: (0, i)),
         scratch_shapes=[
-            pltpu.VMEM((accounts, option_rows), jnp.bfloat16),
             pltpu.VMEM((option_rows, chunk), jnp.bfloat16),
             pltpu.VMEM((3 * places, chunk), jnp.bfloat16),
             pltpu.VMEM((3 * places, chunk), jnp.bfloat16),
             pltpu.VMEM((places, chunk), jnp.bfloat16),
             pltpu.VMEM((places, chunk), jnp.bfloat16),
         ],
-        compiler_params=pltpu.CompilerParams(vmem_limit_bytes=40 * 1024 * 1024),
-    )(factor_returns, loads, base, expand, params, positions)
-    losses = lax.psum_scatter(partial, "inst", scatter_dimension=0, tiled=True).astype(f32)
+        compiler_params=pltpu.CompilerParams(vmem_limit_bytes=24 * 1024 * 1024),
+        cost_estimate=pl.CostEstimate(
+            flops=60 * option_rows * piece * 64, bytes_accessed=8 << 20, transcendentals=0
+        ),
+    )
+    sums = []
+    for at in range(pieces):
+        part = price(
+            factor_returns[at * piece : (at + 1) * piece], loads, base, expand, params, held
+        )
+        sums.append(lax.psum_scatter(part, "inst", scatter_dimension=0, tiled=True))
+    losses = jnp.concatenate(sums, axis=1).astype(f32)
     margin = lax.pmax(jnp.max(losses, axis=1), "scen")
     return (losses, margin)
 

time: 116 us -> 145 us (1.25)
  waiting for transfers between devices: 48.1 us -> 65 us
  local copies, waits for them, and re-layouts: 4.6 us -> 12.4 us
  other arithmetic: 5.17 us -> 11.9 us
  blocking collectives: 14 us -> 12.4 us
    reduce_scatter x1 -> x4, waiting for transfers between devices: 42.7 us -> 63.6 us  [body(): sums.append(lax.psum_scatter(part, 'inst', scatter_dimension=0, tiled=True))]
    unnamed x15 -> x38, local copies, waits for them, and re-layouts: 2.41 us -> 9.52 us
    convert_element_type x0 -> x2, other arithmetic: none -> 5.01 us  [the longest x1 2.83 us: body(): held = (contract_size * positions.astype(f32)).astype(jnp.bfloat16)]
    all_to_all x1, waiting for transfers between devices: 5.38 us -> 1.32 us  [body(): lax.all_to_all(send.reshape(n_inst, CAP, 256), 'inst', split_axis=0, conc...]
    reduce_max x1 -> x5, other arithmetic: 2.35 us -> 4.08 us  [body(): margin = lax.pmax(jnp.max(losses, axis=1), 'scen')]
    pmax x1, blocking collectives: 14 us -> 12.4 us  [body(): margin = lax.pmax(jnp.max(losses, axis=1), 'scen')]
    pallas_call x1 -> x4, Pallas kernels: 21.3 us -> 20.1 us  [body(): price(factor_returns[at * piece:(at + 1) * piece], loads, base, expand, p...]
  transfers between devices with their start and end apart: 2 -> 5, of which waited for: 2 -> 4; matrix products, arithmetic and copies ran while one was open for 0% -> 7% of each run, Pallas kernels for 0% -> 10%
where the time goes in v2:
time: 145 us; the launch traced here: 144 us
  waiting for transfers between devices  65 us (45%)
  Pallas kernels  20.1 us (14%)
  between operations  14.1 us (10%)
  local copies, waits for them, and re-layouts  12.4 us (9%)
  blocking collectives  12.4 us (9%)
  other arithmetic  11.9 us (8%)
  starting transfers between devices  6.44 us (4%)
  matrix products  1.95 us (1%)
    reduce_scatter x4, waiting for transfers between devices, body(): sums.append(lax.psum_scatter(part, 'inst', scatter_dimension=0, tiled=True))  63.6 us
    pallas_call x4, Pallas kernels, body(): price(factor_returns[at * piece:(at + 1) * piece], loads, base, expand, p...  20.1 us
    pmax x1, blocking collectives, body(): margin = lax.pmax(jnp.max(losses, axis=1), 'scen')  12.4 us
    unnamed x38, local copies, waits for them, and re-layouts  9.52 us
    all_to_all x1, starting transfers between devices, body(): lax.all_to_all(send.reshape(n_inst, CAP, 256), 'inst', split_axis=0, conc...  6.32 us
    reduce_max x5, other arithmetic, body(): margin = lax.pmax(jnp.max(losses, axis=1), 'scen')  4.08 us
  transfers between devices with their start and end apart: 5, of which 4 were waited for; matrix products, arithmetic and copies ran while one was open for 7% of the time, Pallas kernels for 10%

profile of v2, /device:TPU:0, one launch (start us, length us, event | category | flops | bytes accessed | tf_op | source)
XLA Modules:
  0.0 144.2 jit_solution(5103602686698919125)
XLA Ops:
  7.2 0.8 add_select_fusion.5
  8.0 0.7 reshape.99
  8.7 0.7 fusion.19
  9.4 0.7 fusion.6
  10.2 0.4 fusion.1
  10.7 0.1 slice_compare_fusion
  10.8 0.1 fusion.39
  10.9 0.1 fusion.13
  11.0 0.2 slice_reduce_fusion
  11.2 0.1 select_reduce_fusion.1
  11.3 0.1 convert_add_fusion
  11.5 0.3 select_reduce_fusion
  11.8 0.1 sub.58
  11.9 0.4 convolution_convert_fusion
  12.3 0.3 convolution_convert_fusion.1
  12.6 0.7 copy.57
  13.4 6.3 %all-to-all-start = ((bf16[4,48,256]{2,1,0:T(8,128)(2,1)}), bf16[4,48,256]{2,1,0:T(8,128)(2,1)S(1)}, u32[]{:S(2)}, u32[]{:S(2)}) async-start(bf16[4,48,256]{2,1,0:T(8,128)(2,1)} %bitcast.6), calls=%async_computation | async-start | bytes 196608 | tf_op jit(solution)/shard_map/all_to_all | solution.py:142
  19.8 2.8 %multiply_convert_fusion.pos_ref = bf16[1024,1024]{1,0:T(8,128)(2,1)S(1)} fusion(s32[1024,1024]{1,0:T(8,128)} %param.15), kind=kLoop, calls=%fused_computation | loop fusion | flops 3145728 | bytes 6291456 | tf_op jit(solution)/shard_map/convert_element_type | solution.py:173
  22.6 0.6 fusion.37
  23.3 0.7 copy.68.fr_ref
  24.0 0.2 fusion.3.expand_ref
  24.2 1.3 all-to-all-done
  25.5 0.4 fusion.2
  26.1 0.2 copy.58.params_ref
  26.3 0.8 copy-done.5
  27.1 5.0 %shard_map.95 = bf16[1024,256]{1,0:T(8,128)(2,1)S(1)} custom-call(bf16[256,64]{1,0:T(8,128)(2,1)S(1)} %copy-done.5, bf16[192,128]{1,0:T(8,128)(2,1)S(1)} %slice.57.loads_ref, bf16[192,2]{1,0:T(8,128)(2,1)S(1)} %slice.58.base_ref, bf16[1024,192]{1,0:T(8,128)(2,1)S(1)} %fusion.3.expand_ref, f32[1024,8]{1,0:T(8,128)S(1)} %copy.58.params_ref, ...), custom_call_target="tpu_custom_call" | custom-call | flops 1006632960 | bytes 8388608 | tf_op jit(solution)/shard_map/pallas_call | solution.py:195
  32.2 0.8 copy-done.1
  33.0 0.7 copy.69.fr_ref
  33.8 0.8 copy-done.7
  34.6 5.0 %shard_map.96 = bf16[1024,256]{1,0:T(8,128)(2,1)S(1)} custom-call(bf16[256,64]{1,0:T(8,128)(2,1)S(1)} %copy-done.7, bf16[192,128]{1,0:T(8,128)(2,1)S(1)} %slice.57.loads_ref, bf16[192,2]{1,0:T(8,128)(2,1)S(1)} %slice.58.base_ref, bf16[1024,192]{1,0:T(8,128)(2,1)S(1)} %fusion.3.expand_ref, f32[1024,8]{1,0:T(8,128)S(1)} %copy.58.params_ref, ...), custom_call_target="tpu_custom_call" | custom-call | flops 1006632960 | bytes 8388608 | tf_op jit(solution)/shard_map/pallas_call | solution.py:195
  39.6 0.8 copy-done.2
  40.5 0.7 copy.70.fr_ref
  41.3 0.8 copy-done.8
  42.1 5.0 %shard_map.97 = bf16[1024,256]{1,0:T(8,128)(2,1)S(1)} custom-call(bf16[256,64]{1,0:T(8,128)(2,1)S(1)} %copy-done.8, bf16[192,128]{1,0:T(8,128)(2,1)S(1)} %slice.57.loads_ref, bf16[192,2]{1,0:T(8,128)(2,1)S(1)} %slice.58.base_ref, bf16[1024,192]{1,0:T(8,128)(2,1)S(1)} %fusion.3.expand_ref, f32[1024,8]{1,0:T(8,128)S(1)} %copy.58.params_ref, ...), custom_call_target="tpu_custom_call" | custom-call | flops 1006632960 | bytes 8388608 | tf_op jit(solution)/shard_map/pallas_call | solution.py:195
  47.1 0.8 copy-done.3
  48.0 0.7 copy.71.fr_ref
  48.8 0.8 copy-done.6
  49.6 5.0 %shard_map.98 = bf16[1024,256]{1,0:T(8,128)(2,1)S(1)} custom-call(bf16[256,64]{1,0:T(8,128)(2,1)S(1)} %copy-done.6, bf16[192,128]{1,0:T(8,128)(2,1)S(1)} %slice.57.loads_ref, bf16[192,2]{1,0:T(8,128)(2,1)S(1)} %slice.58.base_ref, bf16[1024,192]{1,0:T(8,128)(2,1)S(1)} %fusion.3.expand_ref, f32[1024,8]{1,0:T(8,128)S(1)} %copy.58.params_ref, ...), custom_call_target="tpu_custom_call" | custom-call | flops 1006632960 | bytes 8388608 | tf_op jit(solution)/shard_map/pallas_call | solution.py:195
  54.6 0.8 copy-done.4
  55.5 1.0 reduce_max.30
  56.5 20.7 %reduce-scatter.7.cloned.1.call-done = bf16[256,256]{1,0:T(8,128)(2,1)} async-done(((bf16[1024,256]{1,0:T(8,128)(2,1)}), bf16[256,256]{1,0:T(8,128)(2,1)}) %reduce-scatter.7.cloned.1.call-update) | async-done | bytes 131088 | tf_op jit(solution)/shard_map/reduce_scatter | solution.py:198
  77.1 1.0 reduce_max.31
  78.2 21.3 %reduce-scatter.9.cloned.1.call-done = bf16[256,256]{1,0:T(8,128)(2,1)} async-done(((bf16[1024,256]{1,0:T(8,128)(2,1)}), bf16[256,256]{1,0:T(8,128)(2,1)}) %reduce-scatter.9.cloned.1.call-update) | async-done | bytes 131088 | tf_op jit(solution)/shard_map/reduce_scatter | solution.py:198
  99.4 1.0 reduce_max.41
  100.5 21.7 %reduce-scatter.11.cloned.1.call-done = bf16[256,256]{1,0:T(8,128)(2,1)} async-done(((bf16[1024,256]{1,0:T(8,128)(2,1)}), bf16[256,256]{1,0:T(8,128)(2,1)}) %reduce-scatter.11.cloned.1.call-update) | async-done | bytes 131088 | tf_op jit(solution)/shard_map/reduce_scatter | solution.py:198
  122.1 1.0 reduce_max.43
  123.2 12.4 %pmax.7 = f32[256]{0:T(256)} all-reduce(f32[256]{0:T(256)S(1)} %maximum_convert_fusion.1), channel_id=1, replica_groups=mesh['inst'=4,'scen'=8] {'scen'}, use_global_device_ids=true, to_apply=%region_12.13 | all-reduce | flops 256 | bytes 2048 | tf_op jit(solution)/shard_map/pmax | solution.py:200
  135.5 2.2 %maximum_convert_fusion = f32[256,1024]{1,0:T(8,128)} fusion(bf16[256,256]{1,0:T(8,128)(2,1)} %reduce-scatter.11.cloned.1.call-done, bf16[256,256]{1,0:T(8,128)(2,1)} %reduce-scatter.9.cloned.1.call-done, bf16[256,256]{1,0:T(8,128)(2,1)} %reduce-scatter.7.cloned.1.call-done, bf16[256,256]{1,0:T(8,128)(2,1)} %reduce-scatter.5.cloned.1.call-done), kind=kLoop, calls=%fused_computation.15 | loop fusion | flops 2097152 | bytes 1572864 | tf_op jit(solution)/shard_map/convert_element_type | solution.py:199
  (57 shorter events, 0.6 us)
Async XLA Ops:
  7.2 4.7 %copy-start = (bf16[1000,128]{1,0:T(8,128)(2,1)S(1)}, bf16[1000,128]{1,0:T(8,128)(2,1)}, u32[]{:S(2)}) copy-start(bf16[1000,128]{1,0:T(8,128)(2,1)} %param.9) | copy-start | bytes 768004
  10.2 2.1 %copy-start.15 = (bf16[2,1000]{1,0:T(2,128)(2,1)S(1)}, bf16[2,1000]{1,0:T(2,128)(2,1)}, u32[]{:S(2)}) copy-start(bf16[2,1000]{1,0:T(2,128)(2,1)} %param.10) | copy-start | bytes 12004
  13.4 12.1 %all-to-all-start = ((bf16[4,48,256]{2,1,0:T(8,128)(2,1)}), bf16[4,48,256]{2,1,0:T(8,128)(2,1)S(1)}, u32[]{:S(2)}, u32[]{:S(2)}) async-start(bf16[4,48,256]{2,1,0:T(8,128)(2,1)} %bitcast.6), calls=%async_computation | async-start | bytes 196608 | tf_op jit(solution)/shard_map/all_to_all | solution.py:142
  19.7 35.8 %reduce-scatter.5.cloned.1.call-start = ((), (), s32[]{:S(2)}) async-start(), calls=%async_computation.5 | async-start | bytes 655360 | tf_op jit(solution)/shard_map/reduce_scatter | solution.py:198
  19.7 2.9 %copy-start.9 = (bf16[1024,64]{0,1:T(8,128)(2,1)S(1)}, bf16[1024,64]{0,1:T(8,128)(2,1)}, u32[]{:S(2)}) copy-start(bf16[1024,64]{0,1:T(8,128)(2,1)} %param.8) | copy-start | bytes 393220
  19.8 6.2 %copy-start.13 = (s32[1024]{0:T(1024)S(1)}, s32[1024]{0:T(1024)}, u32[]{:S(2)}) copy-start(s32[1024]{0:T(1024)} %param.13) | copy-start | bytes 12292
  19.8 6.2 %copy-start.14 = (f32[1024]{0:T(1024)S(1)}, f32[1024]{0:T(1024)}, u32[]{:S(2)}) copy-start(f32[1024]{0:T(1024)} %param.14) | copy-start | bytes 12292
  26.3 0.8 copy-start.5
  27.1 5.9 %copy-start.12 = (bf16[256,64]{0,1:T(8,128)(2,1)S(1)}, bf16[256,64]{0,1:T(8,128)(2,1)}, u32[]{:S(2)}) copy-start(bf16[256,64]{0,1:T(8,128)(2,1)} %get-tuple-element.8) | copy-start | bytes 98308
  32.1 0.8 copy-start.1
  33.0 44.2 %reduce-scatter.7.cloned.1.call-start = ((), (), s32[]{:S(2)}) async-start(), calls=%async_computation.6 | async-start | bytes 655360 | tf_op jit(solution)/shard_map/reduce_scatter | solution.py:198
  33.7 0.8 copy-start.7
  34.6 5.9 %copy-start.11 = (bf16[256,64]{0,1:T(8,128)(2,1)S(1)}, bf16[256,64]{0,1:T(8,128)(2,1)}, u32[]{:S(2)}) copy-start(bf16[256,64]{0,1:T(8,128)(2,1)} %get-tuple-element.7) | copy-start | bytes 98308
  39.6 0.8 copy-start.2
  40.5 59.0 %reduce-scatter.9.cloned.1.call-start = ((), (), s32[]{:S(2)}) async-start(), calls=%async_computation.7 | async-start | bytes 655360 | tf_op jit(solution)/shard_map/reduce_scatter | solution.py:198
  41.2 0.8 copy-start.8
  42.1 5.9 %copy-start.10 = (bf16[256,64]{0,1:T(8,128)(2,1)S(1)}, bf16[256,64]{0,1:T(8,128)(2,1)}, u32[]{:S(2)}) copy-start(bf16[256,64]{0,1:T(8,128)(2,1)} %get-tuple-element.9) | copy-start | bytes 98308
  47.1 0.8 copy-start.3
  48.0 74.2 %reduce-scatter.11.cloned.1.call-start = ((), (), s32[]{:S(2)}) async-start(), calls=%async_computation.8 | async-start | bytes 655360 | tf_op jit(solution)/shard_map/reduce_scatter | solution.py:198
  48.8 0.8 copy-start.6
  54.6 0.8 copy-start.4
Sparse Core Ops, SparseCore 0:
  33.1 21.8 reduce-scatter.4
  57.2 19.8 reduce-scatter.6
  79.4 19.9 reduce-scatter.8
  102.1 19.9 reduce-scatter.10

commit v3 on v2

--- a/solution.py
+++ b/solution.py
@@ -116,6 +116,21 @@
 
     lax.fori_loop(0, options // tile, step, 0)
     out_ref[...] = jnp.dot(pos_ref[...], pnl[...], preferred_element_type=f32).astype(out_ref.dtype)
+
+
+def halving_sum(part, axis, myself, count):
+    left = part.reshape(count, part.shape[0] // count, part.shape[1])
+    bit = 1
+    while bit < count:
+        halves = left.reshape(left.shape[0] // 2, 2, left.shape[1], left.shape[2])
+        mine = (myself // bit) % 2
+        keep = lax.dynamic_index_in_dim(halves, mine, 1, keepdims=False)
+        give = lax.dynamic_index_in_dim(halves, 1 - mine, 1, keepdims=False)
+        pairs = [(i, i ^ bit) for i in range(count)]
+        got = lax.ppermute(give.astype(jnp.bfloat16), axis, pairs)
+        left = keep.astype(jnp.float32) + got.astype(jnp.float32)
+        bit *= 2
+    return left[0]
 
 
 def body(
@@ -195,9 +210,15 @@
         part = price(
             factor_returns[at * piece : (at + 1) * piece], loads, base, expand, params, held
         )
-        sums.append(lax.psum_scatter(part, "inst", scatter_dimension=0, tiled=True))
-    losses = jnp.concatenate(sums, axis=1).astype(f32)
-    margin = lax.pmax(jnp.max(losses, axis=1), "scen")
+        sums.append(halving_sum(part, "inst", myself, n_inst))
+    losses = jnp.concatenate(sums, axis=1)
+    margin = functools.reduce(jnp.maximum, [jnp.max(one, axis=1) for one in sums])
+    n_scen = lax.axis_size("scen")
+    bit = 1
+    while bit < n_scen:
+        pairs = [(i, i ^ bit) for i in range(n_scen)]
+        margin = jnp.maximum(margin, lax.ppermute(margin, "scen", pairs))
+        bit *= 2
     return (losses, margin)
 
 

time: 145 us -> 80.8 us (0.56)
  waiting for transfers between devices: 65 us -> 23 us
  starting transfers between devices: 6.44 us -> 19.8 us
  between operations: 14.1 us -> 1.14 us
  blocking collectives: 12.4 us -> 0 us
  local copies, waits for them, and re-layouts: 12.4 us -> 6.2 us
  other arithmetic: 11.9 us -> 8.04 us
    reduce_scatter x4 -> x0, waiting for transfers between devices: 63.6 us -> none  [body(): sums.append(lax.psum_scatter(part, 'inst', scatter_dimension=0, tiled=True))]
    ppermute x0 -> x11, waiting for transfers between devices: none -> 23 us  [the longest x8 18.8 us: halving_sum(): got = lax.ppermute(give.astype(jnp.bfloat16), axis, pairs)]
    ppermute x0 -> x11, starting transfers between devices: none -> 13.5 us  [the longest x8 10.4 us: halving_sum(): got = lax.ppermute(give.astype(jnp.bfloat16), axis, pairs)]
    pmax x1 -> x0, blocking collectives: 12.4 us -> none  [body(): margin = lax.pmax(jnp.max(losses, axis=1), 'scen')]
    unnamed x38 -> x24, local copies, waits for them, and re-layouts: 9.52 us -> 3.8 us
    reduce_max x5 -> x4, other arithmetic: 4.08 us -> 0.48 us  [body(): jnp.max(one, axis=1)]
    convert_element_type x1 -> x0, other arithmetic: 2.18 us -> none  [body(): losses = jnp.concatenate(sums, axis=1).astype(f32)]
  transfers between devices with their start and end apart: 5 -> 12, of which waited for: 4 -> 7; matrix products, arithmetic and copies ran while one was open for 7% -> 10% of each run, Pallas kernels for 10% -> 19%
where the time goes in v3:
time: 80.8 us; the launch traced here: 80.4 us
  waiting for transfers between devices  23 us (28%)
  Pallas kernels  20.2 us (25%)
  starting transfers between devices  19.8 us (25%)
  other arithmetic  8.04 us (10%)
  local copies, waits for them, and re-layouts  6.2 us (8%)
  matrix products  1.95 us (2%)
  between operations  1.14 us (1%)
    pallas_call x4, Pallas kernels, body(): price(factor_returns[at * piece:(at + 1) * piece], loads, base, expand, p...  20.2 us
    ppermute x8, waiting for transfers between devices, halving_sum(): got = lax.ppermute(give.astype(jnp.bfloat16), axis, pairs)  18.8 us
    ppermute x8, starting transfers between devices, halving_sum(): got = lax.ppermute(give.astype(jnp.bfloat16), axis, pairs)  10.4 us
    all_to_all x1, starting transfers between devices, body(): lax.all_to_all(send.reshape(n_inst, CAP, 256), 'inst', split_axis=0, conc...  6.32 us
    ppermute x3, waiting for transfers between devices, body(): margin = jnp.maximum(margin, lax.ppermute(margin, 'scen', pairs))  4.16 us
    unnamed x24, local copies, waits for them, and re-layouts  3.8 us
    ppermute x3, starting transfers between devices, body(): margin = jnp.maximum(margin, lax.ppermute(margin, 'scen', pairs))  3.08 us
    convert_element_type x1, other arithmetic, body(): held = (contract_size * positions.astype(f32)).astype(jnp.bfloat16)  2.84 us
  transfers between devices with their start and end apart: 12, of which 7 were waited for; matrix products, arithmetic and copies ran while one was open for 10% of the time, Pallas kernels for 19%

profile of v3, /device:TPU:0, one launch (start us, length us, event | category | flops | bytes accessed | tf_op | source)
XLA Modules:
  0.0 80.4 jit_solution(17239939428467001539)
XLA Ops:
  0.6 0.8 add_select_fusion.5
  1.4 0.7 reshape.135
  2.2 0.7 fusion.27
  2.9 0.7 fusion.6
  3.7 0.4 fusion.1
  4.3 0.1 fusion.21
  4.5 0.2 slice_reduce_fusion
  4.7 0.1 select_reduce_fusion.1
  4.8 0.1 convert_add_fusion.8
  5.0 0.3 select_reduce_fusion
  5.4 0.4 convolution_convert_fusion
  5.8 0.3 convolution_convert_fusion.1
  6.1 0.7 copy.77
  6.8 6.3 %all-to-all-start = ((bf16[4,48,256]{2,1,0:T(8,128)(2,1)}), bf16[4,48,256]{2,1,0:T(8,128)(2,1)S(1)}, u32[]{:S(2)}, u32[]{:S(2)}) async-start(bf16[4,48,256]{2,1,0:T(8,128)(2,1)} %bitcast.6), calls=%async_computation | async-start | bytes 196608 | tf_op jit(solution)/shard_map/all_to_all | solution.py:157
  13.3 2.8 %multiply_convert_fusion.pos_ref = bf16[1024,1024]{1,0:T(8,128)(2,1)S(1)} fusion(s32[1024,1024]{1,0:T(8,128)} %param.15), kind=kLoop, calls=%fused_computation | loop fusion | flops 3145728 | bytes 6291456 | tf_op jit(solution)/shard_map/convert_element_type | solution.py:188
  16.2 0.7 copy.92.fr_ref
  16.9 0.7 copy.94.fr_ref
  17.6 0.7 copy.96.fr_ref
  18.3 0.7 copy.98.fr_ref
  19.1 0.2 fusion.3.expand_ref
  19.3 0.4 fusion.2
  19.8 0.2 copy.78.params_ref
  20.0 0.8 %copy-done.4 = bf16[256,64]{1,0:T(8,128)(2,1)S(1)} copy-done((bf16[256,64]{1,0:T(8,128)(2,1)S(1)}, bf16[256,64]{1,0:T(8,128)(2,1)}, u32[]{:S(2)}) %copy-start.4) | copy-done | bytes 32792
  20.9 5.1 %shard_map.95 = bf16[1024,256]{1,0:T(8,128)(2,1)S(1)} custom-call(bf16[256,64]{1,0:T(8,128)(2,1)S(1)} %copy-done.4, bf16[192,128]{1,0:T(8,128)(2,1)S(1)} %slice.57.loads_ref, bf16[192,2]{1,0:T(8,128)(2,1)S(1)} %slice.58.base_ref, bf16[1024,192]{1,0:T(8,128)(2,1)S(1)} %fusion.3.expand_ref, f32[1024,8]{1,0:T(8,128)S(1)} %copy.78.params_ref, ...), custom_call_target="tpu_custom_call" | custom-call | flops 1006632960 | bytes 8388608 | tf_op jit(solution)/shard_map/pallas_call | solution.py:210
  26.0 2.1 %collective-permute-start = (bf16[2,256,256]{2,1,0:T(8,128)(2,1)S(1)}, bf16[2,256,256]{2,1,0:T(8,128)(2,1)S(1)}, u32[]{:S(2)}, u32[]{:S(2)}) collective-permute-start(bf16[2,256,256]{2,1,0:T(8,128)(2,1)S(1)} %dynamic-slice_bitcast_fusion.3), channel_id=1, source_target_pairs={{0,8},{8,0},{16,24},{24,16},{1,9},{9,1},{17,25},{25,17},{2,10},{10... | collective-permute-start | bytes 786440 | tf_op jit(solution)/shard_map/ppermute | solution.py:130
  28.1 5.1 %shard_map.96 = bf16[1024,256]{1,0:T(8,128)(2,1)S(1)} custom-call(bf16[256,64]{1,0:T(8,128)(2,1)S(1)} %copy-done.3, bf16[192,128]{1,0:T(8,128)(2,1)S(1)} %slice.57.loads_ref, bf16[192,2]{1,0:T(8,128)(2,1)S(1)} %slice.58.base_ref, bf16[1024,192]{1,0:T(8,128)(2,1)S(1)} %fusion.3.expand_ref, f32[1024,8]{1,0:T(8,128)S(1)} %copy.78.params_ref, ...), custom_call_target="tpu_custom_call" | custom-call | flops 1006632960 | bytes 8388608 | tf_op jit(solution)/shard_map/pallas_call | solution.py:210
  33.3 5.1 %shard_map.97 = bf16[1024,256]{1,0:T(8,128)(2,1)S(1)} custom-call(bf16[256,64]{1,0:T(8,128)(2,1)S(1)} %copy-done.2, bf16[192,128]{1,0:T(8,128)(2,1)S(1)} %slice.57.loads_ref, bf16[192,2]{1,0:T(8,128)(2,1)S(1)} %slice.58.base_ref, bf16[1024,192]{1,0:T(8,128)(2,1)S(1)} %fusion.3.expand_ref, f32[1024,8]{1,0:T(8,128)S(1)} %copy.78.params_ref, ...), custom_call_target="tpu_custom_call" | custom-call | flops 1006632960 | bytes 8388608 | tf_op jit(solution)/shard_map/pallas_call | solution.py:210
  38.4 2.1 %collective-permute-start.4 = (bf16[2,256,256]{2,1,0:T(8,128)(2,1)S(1)}, bf16[2,256,256]{2,1,0:T(8,128)(2,1)S(1)}, u32[]{:S(2)}, u32[]{:S(2)}) collective-permute-start(bf16[2,256,256]{2,1,0:T(8,128)(2,1)S(1)} %dynamic-slice_bitcast_fusion.1), channel_id=1, source_target_pairs={{0,8},{8,0},{16,24},{24,16},{1,9},{9,1},{17,25},{25,17},{2,10},{10... | collective-permute-start | bytes 786440 | tf_op jit(solution)/shard_map/ppermute | solution.py:130
  40.4 5.1 %shard_map.98 = bf16[1024,256]{1,0:T(8,128)(2,1)S(1)} custom-call(bf16[256,64]{1,0:T(8,128)(2,1)S(1)} %copy-done.1, bf16[192,128]{1,0:T(8,128)(2,1)S(1)} %slice.57.loads_ref, bf16[192,2]{1,0:T(8,128)(2,1)S(1)} %slice.58.base_ref, bf16[1024,192]{1,0:T(8,128)(2,1)S(1)} %fusion.3.expand_ref, f32[1024,8]{1,0:T(8,128)S(1)} %copy.78.params_ref, ...), custom_call_target="tpu_custom_call" | custom-call | flops 1006632960 | bytes 8388608 | tf_op jit(solution)/shard_map/pallas_call | solution.py:210
  45.5 0.1 collective-permute-start.6
  45.7 3.0 %collective-permute-start.1 = (bf16[1,256,256]{2,1,0:T(8,128)(2,1)S(1)}, bf16[1,256,256]{2,1,0:T(8,128)(2,1)S(1)}, u32[]{:S(2)}, u32[]{:S(2)}) collective-permute-start(bf16[1,256,256]{2,1,0:T(8,128)(2,1)S(1)} %dynamic-slice_convert_fusion.3), channel_id=1, source_target_pairs={{0,16},{8,24},{16,0},{24,8},{1,17},{9,25},{17,1},{25,9},{2,18},{10... | collective-permute-start | bytes 393224 | tf_op jit(solution)/shard_map/ppermute | solution.py:130
  48.8 0.1 collective-permute-start.3
  49.0 3.0 %collective-permute-start.5 = (bf16[1,256,256]{2,1,0:T(8,128)(2,1)S(1)}, bf16[1,256,256]{2,1,0:T(8,128)(2,1)S(1)}, u32[]{:S(2)}, u32[]{:S(2)}) collective-permute-start(bf16[1,256,256]{2,1,0:T(8,128)(2,1)S(1)} %dynamic-slice_convert_fusion.1), channel_id=1, source_target_pairs={{0,16},{8,24},{16,0},{24,8},{1,17},{9,25},{17,1},{25,9},{2,18},{10... | collective-permute-start | bytes 393224 | tf_op jit(solution)/shard_map/ppermute | solution.py:130
  51.9 5.6 %collective-permute-done.6 = bf16[2,256,256]{2,1,0:T(8,128)(2,1)S(1)} collective-permute-done((bf16[2,256,256]{2,1,0:T(8,128)(2,1)S(1)}, bf16[2,256,256]{2,1,0:T(8,128)(2,1)S(1)}, u32[]{:S(2)}, u32[]{:S(2)}) %collective-permute-start.6) | collective-permute-done | bytes 262176 | tf_op jit(solution)/shard_map/ppermute | solution.py:130
  57.7 0.1 fusion.11
  57.8 9.3 %collective-permute-done.3 = bf16[1,256,256]{2,1,0:T(8,128)(2,1)S(1)} collective-permute-done((bf16[1,256,256]{2,1,0:T(8,128)(2,1)S(1)}, bf16[1,256,256]{2,1,0:T(8,128)(2,1)S(1)}, u32[]{:S(2)}, u32[]{:S(2)}) %collective-permute-start.3) | collective-permute-done | bytes 131104 | tf_op jit(solution)/shard_map/ppermute | solution.py:130
  67.1 0.1 fusion.13
  67.3 2.7 %collective-permute-done.5 = bf16[1,256,256]{2,1,0:T(8,128)(2,1)S(1)} collective-permute-done((bf16[1,256,256]{2,1,0:T(8,128)(2,1)S(1)}, bf16[1,256,256]{2,1,0:T(8,128)(2,1)S(1)}, u32[]{:S(2)}, u32[]{:S(2)}) %collective-permute-start.5) | collective-permute-done | bytes 131104 | tf_op jit(solution)/shard_map/ppermute | solution.py:130
  69.9 0.1 fusion.15
  70.0 1.3 %collective-permute-done.7 = bf16[1,256,256]{2,1,0:T(8,128)(2,1)S(1)} collective-permute-done((bf16[1,256,256]{2,1,0:T(8,128)(2,1)S(1)}, bf16[1,256,256]{2,1,0:T(8,128)(2,1)S(1)}, u32[]{:S(2)}, u32[]{:S(2)}) %collective-permute-start.7) | collective-permute-done | bytes 131104 | tf_op jit(solution)/shard_map/ppermute | solution.py:130
  71.3 0.1 fusion.17
  71.5 1.1 %collective-permute-done.8 = f32[256]{0:T(256)S(1)} collective-permute-done((f32[256]{0:T(256)S(1)}, f32[256]{0:T(256)S(1)}, u32[]{:S(2)}, u32[]{:S(2)}) %collective-permute-start.8) | collective-permute-done | bytes 1056 | tf_op jit(solution)/shard_map/ppermute | solution.py:220
  72.7 1.5 %collective-permute-start.9 = (f32[256]{0:T(256)S(1)}, f32[256]{0:T(256)S(1)}, u32[]{:S(2)}, u32[]{:S(2)}) collective-permute-start(f32[256]{0:T(256)S(1)} %max.21), channel_id=1, source_target_pairs={{0,2},{1,3},{2,0},{3,1},{4,6},{5,7},{6,4},{7,5},{8,10},{9,11},{10,... | collective-permute-start | bytes 3080 | tf_op jit(solution)/shard_map/ppermute | solution.py:220
  74.2 2.1 %collective-permute-done.9 = f32[256]{0:T(256)S(1)} collective-permute-done((f32[256]{0:T(256)S(1)}, f32[256]{0:T(256)S(1)}, u32[]{:S(2)}, u32[]{:S(2)}) %collective-permute-start.9) | collective-permute-done | bytes 1056 | tf_op jit(solution)/shard_map/ppermute | solution.py:220
  76.2 1.5 %collective-permute-start.10 = (f32[256]{0:T(256)S(1)}, f32[256]{0:T(256)S(1)}, u32[]{:S(2)}, u32[]{:S(2)}) collective-permute-start(f32[256]{0:T(256)S(1)} %max.22), channel_id=1, source_target_pairs={{0,4},{1,5},{2,6},{3,7},{4,0},{5,1},{6,2},{7,3},{8,12},{9,13},{10,... | collective-permute-start | bytes 3080 | tf_op jit(solution)/shard_map/ppermute | solution.py:220
  77.8 1.1 %pad_maximum_fusion = f32[256,1024]{1,0:T(8,128)} fusion(f32[256,256]{1,0:T(8,128)S(1)} %get-tuple-element.13, f32[256,256]{1,0:T(8,128)S(1)} %get-tuple-element.11, f32[256,256]{1,0:T(8,128)S(1)} %get-tuple-element.7, f32[256,256]{1,0:T(8,128)S(1)} %get-tuple-element.9), kind=kLoop, calls=%fused_computation.8 | loop fusion | flops 786432 | bytes 2097152 | tf_op jit(solution)/shard_map/concatenate | solution.py:214
  78.9 1.0 %collective-permute-done.10 = f32[256]{0:T(256)S(1)} collective-permute-done((f32[256]{0:T(256)S(1)}, f32[256]{0:T(256)S(1)}, u32[]{:S(2)}, u32[]{:S(2)}) %collective-permute-start.10) | collective-permute-done | bytes 1056 | tf_op jit(solution)/shard_map/ppermute | solution.py:220
  79.8 0.6 max.23
  (67 shorter events, 1.3 us)
Async XLA Ops:
  0.6 4.7 %copy-start = (bf16[1000,128]{1,0:T(8,128)(2,1)S(1)}, bf16[1000,128]{1,0:T(8,128)(2,1)}, u32[]{:S(2)}) copy-start(bf16[1000,128]{1,0:T(8,128)(2,1)} %param.9) | copy-start | bytes 768004
  3.7 2.1 %copy-start.8 = (bf16[2,1000]{1,0:T(2,128)(2,1)S(1)}, bf16[2,1000]{1,0:T(2,128)(2,1)}, u32[]{:S(2)}) copy-start(bf16[2,1000]{1,0:T(2,128)(2,1)} %param.10) | copy-start | bytes 12004
  6.8 12.4 %all-to-all-start = ((bf16[4,48,256]{2,1,0:T(8,128)(2,1)}), bf16[4,48,256]{2,1,0:T(8,128)(2,1)S(1)}, u32[]{:S(2)}, u32[]{:S(2)}) async-start(bf16[4,48,256]{2,1,0:T(8,128)(2,1)} %bitcast.6), calls=%async_computation | async-start | bytes 196608 | tf_op jit(solution)/shard_map/all_to_all | solution.py:157
  13.2 2.9 %copy-start.5 = (bf16[1024,64]{0,1:T(8,128)(2,1)S(1)}, bf16[1024,64]{0,1:T(8,128)(2,1)}, u32[]{:S(2)}) copy-start(bf16[1024,64]{0,1:T(8,128)(2,1)} %param.8) | copy-start | bytes 393220
  13.3 6.4 %copy-start.6 = (s32[1024]{0:T(1024)S(1)}, s32[1024]{0:T(1024)}, u32[]{:S(2)}) copy-start(s32[1024]{0:T(1024)} %param.13) | copy-start | bytes 12292
  13.3 6.4 %copy-start.7 = (f32[1024]{0:T(1024)S(1)}, f32[1024]{0:T(1024)}, u32[]{:S(2)}) copy-start(f32[1024]{0:T(1024)} %param.14) | copy-start | bytes 12292
  20.0 0.8 %copy-start.4 = (bf16[256,64]{1,0:T(8,128)(2,1)S(1)}, bf16[256,64]{1,0:T(8,128)(2,1)}, u32[]{:S(2)}) copy-start(bf16[256,64]{1,0:T(8,128)(2,1)} %copy.92.fr_ref) | copy-start | bytes 98308
  20.9 7.2 %copy-start.3 = (bf16[256,64]{1,0:T(8,128)(2,1)S(1)}, bf16[256,64]{1,0:T(8,128)(2,1)}, u32[]{:S(2)}) copy-start(bf16[256,64]{1,0:T(8,128)(2,1)} %copy.94.fr_ref) | copy-start | bytes 98308
  26.0 7.3 %copy-start.2 = (bf16[256,64]{1,0:T(8,128)(2,1)S(1)}, bf16[256,64]{1,0:T(8,128)(2,1)}, u32[]{:S(2)}) copy-start(bf16[256,64]{1,0:T(8,128)(2,1)} %copy.96.fr_ref) | copy-start | bytes 98308
  26.0 19.6 %collective-permute-start = (bf16[2,256,256]{2,1,0:T(8,128)(2,1)S(1)}, bf16[2,256,256]{2,1,0:T(8,128)(2,1)S(1)}, u32[]{:S(2)}, u32[]{:S(2)}) collective-permute-start(bf16[2,256,256]{2,1,0:T(8,128)(2,1)S(1)} %dynamic-slice_bitcast_fusion.3), channel_id=1, source_target_pairs={{0,8},{8,0},{16,24},{24,16},{1,9},{9,1},{17,25},{25,17},{2,10},{10... | collective-permute-start | bytes 786440 | tf_op jit(solution)/shard_map/ppermute | solution.py:130
  33.2 7.3 %copy-start.1 = (bf16[256,64]{1,0:T(8,128)(2,1)S(1)}, bf16[256,64]{1,0:T(8,128)(2,1)}, u32[]{:S(2)}) copy-start(bf16[256,64]{1,0:T(8,128)(2,1)} %copy.98.fr_ref) | copy-start | bytes 98308
  33.2 15.5 %collective-permute-start.2 = (bf16[2,256,256]{2,1,0:T(8,128)(2,1)S(1)}, bf16[2,256,256]{2,1,0:T(8,128)(2,1)S(1)}, u32[]{:S(2)}, u32[]{:S(2)}) collective-permute-start(bf16[2,256,256]{2,1,0:T(8,128)(2,1)S(1)} %dynamic-slice_bitcast_fusion.2), channel_id=1, source_target_pairs={{0,8},{8,0},{16,24},{24,16},{1,9},{9,1},{17,25},{25,17},{2,10},{10... | collective-permute-start | bytes 786440 | tf_op jit(solution)/shard_map/ppermute | solution.py:130
  38.4 10.5 %collective-permute-start.4 = (bf16[2,256,256]{2,1,0:T(8,128)(2,1)S(1)}, bf16[2,256,256]{2,1,0:T(8,128)(2,1)S(1)}, u32[]{:S(2)}, u32[]{:S(2)}) collective-permute-start(bf16[2,256,256]{2,1,0:T(8,128)(2,1)S(1)} %dynamic-slice_bitcast_fusion.1), channel_id=1, source_target_pairs={{0,8},{8,0},{16,24},{24,16},{1,9},{9,1},{17,25},{25,17},{2,10},{10... | collective-permute-start | bytes 786440 | tf_op jit(solution)/shard_map/ppermute | solution.py:130
  45.5 12.0 %collective-permute-start.6 = (bf16[2,256,256]{2,1,0:T(8,128)(2,1)S(1)}, bf16[2,256,256]{2,1,0:T(8,128)(2,1)S(1)}, u32[]{:S(2)}, u32[]{:S(2)}) collective-permute-start(bf16[2,256,256]{2,1,0:T(8,128)(2,1)S(1)} %dynamic-slice_bitcast_fusion), channel_id=1, source_target_pairs={{0,8},{8,0},{16,24},{24,16},{1,9},{9,1},{17,25},{25,17},{2,10},{10... | collective-permute-start | bytes 786440 | tf_op jit(solution)/shard_map/ppermute | solution.py:130
  45.7 12.0 %collective-permute-start.1 = (bf16[1,256,256]{2,1,0:T(8,128)(2,1)S(1)}, bf16[1,256,256]{2,1,0:T(8,128)(2,1)S(1)}, u32[]{:S(2)}, u32[]{:S(2)}) collective-permute-start(bf16[1,256,256]{2,1,0:T(8,128)(2,1)S(1)} %dynamic-slice_convert_fusion.3), channel_id=1, source_target_pairs={{0,16},{8,24},{16,0},{24,8},{1,17},{9,25},{17,1},{25,9},{2,18},{10... | collective-permute-start | bytes 393224 | tf_op jit(solution)/shard_map/ppermute | solution.py:130
  48.8 18.4 %collective-permute-start.3 = (bf16[1,256,256]{2,1,0:T(8,128)(2,1)S(1)}, bf16[1,256,256]{2,1,0:T(8,128)(2,1)S(1)}, u32[]{:S(2)}, u32[]{:S(2)}) collective-permute-start(bf16[1,256,256]{2,1,0:T(8,128)(2,1)S(1)} %dynamic-slice_convert_fusion.2), channel_id=1, source_target_pairs={{0,16},{8,24},{16,0},{24,8},{1,17},{9,25},{17,1},{25,9},{2,18},{10... | collective-permute-start | bytes 393224 | tf_op jit(solution)/shard_map/ppermute | solution.py:130
  49.0 21.0 %collective-permute-start.5 = (bf16[1,256,256]{2,1,0:T(8,128)(2,1)S(1)}, bf16[1,256,256]{2,1,0:T(8,128)(2,1)S(1)}, u32[]{:S(2)}, u32[]{:S(2)}) collective-permute-start(bf16[1,256,256]{2,1,0:T(8,128)(2,1)S(1)} %dynamic-slice_convert_fusion.1), channel_id=1, source_target_pairs={{0,16},{8,24},{16,0},{24,8},{1,17},{9,25},{17,1},{25,9},{2,18},{10... | collective-permute-start | bytes 393224 | tf_op jit(solution)/shard_map/ppermute | solution.py:130
  57.6 13.7 %collective-permute-start.7 = (bf16[1,256,256]{2,1,0:T(8,128)(2,1)S(1)}, bf16[1,256,256]{2,1,0:T(8,128)(2,1)S(1)}, u32[]{:S(2)}, u32[]{:S(2)}) collective-permute-start(bf16[1,256,256]{2,1,0:T(8,128)(2,1)S(1)} %dynamic-slice_convert_fusion), channel_id=1, source_target_pairs={{0,16},{8,24},{16,0},{24,8},{1,17},{9,25},{17,1},{25,9},{2,18},{10... | collective-permute-start | bytes 393224 | tf_op jit(solution)/shard_map/ppermute | solution.py:130
  71.5 1.2 %collective-permute-start.8 = (f32[256]{0:T(256)S(1)}, f32[256]{0:T(256)S(1)}, u32[]{:S(2)}, u32[]{:S(2)}) collective-permute-start(f32[256]{0:T(256)S(1)} %maximum_maximum_fusion), channel_id=1, source_target_pairs={{0,1},{1,0},{2,3},{3,2},{4,5},{5,4},{6,7},{7,6},{8,9},{9,8},{10,11... | collective-permute-start | bytes 3080 | tf_op jit(solution)/shard_map/ppermute | solution.py:220
  72.7 3.6 %collective-permute-start.9 = (f32[256]{0:T(256)S(1)}, f32[256]{0:T(256)S(1)}, u32[]{:S(2)}, u32[]{:S(2)}) collective-permute-start(f32[256]{0:T(256)S(1)} %max.21), channel_id=1, source_target_pairs={{0,2},{1,3},{2,0},{3,1},{4,6},{5,7},{6,4},{7,5},{8,10},{9,11},{10,... | collective-permute-start | bytes 3080 | tf_op jit(solution)/shard_map/ppermute | solution.py:220
  76.2 3.6 %collective-permute-start.10 = (f32[256]{0:T(256)S(1)}, f32[256]{0:T(256)S(1)}, u32[]{:S(2)}, u32[]{:S(2)}) collective-permute-start(f32[256]{0:T(256)S(1)} %max.22), channel_id=1, source_target_pairs={{0,4},{1,5},{2,6},{3,7},{4,0},{5,1},{6,2},{7,3},{8,12},{9,13},{10,... | collective-permute-start | bytes 3080 | tf_op jit(solution)/shard_map/ppermute | solution.py:220

commit v4 on v1

--- a/solution.py
+++ b/solution.py
@@ -73,13 +73,58 @@
     return send_row, my_owner * CAP + rank_here
 
 
-def price_kernel(fr_ref, loads_ref, base_ref, expand_ref, params_ref, pos_ref, out_ref, held, pnl, lf_sc, rv_sc, f_sc, v_sc):
+def price_kernel(n, stages, pieces, fr_ref, loads_ref, base_ref, expand_ref, params_ref, pos_ref, out_ref, pnl, lf_sc, rv_sc, f_sc, v_sc, part, send_sem, recv_sem, *buffers):
+    recv, give, keep = buffers[:stages], buffers[stages : 2 * stages - 1], buffers[2 * stages - 1 :]
+    piece = pl.program_id(0)
+    me = lax.axis_index("inst")
+    bits = [(me // (1 << s)) % 2 for s in range(stages)]
+    partners = [me + (1 << s) * (1 - 2 * bits[s]) for s in range(stages)]
+    rows_out, chunk = out_ref.shape[0], fr_ref.shape[0]
+
+    @pl.when(piece == 0)
+    def _():
+        barrier = pltpu.get_barrier_semaphore()
+        for partner in partners:
+            pl.semaphore_signal(
+                barrier, inc=1, device_id={"inst": partner}, device_id_type=pl.DeviceIdType.MESH
+            )
+        pl.semaphore_wait(barrier, stages)
+
+    def copy(s, j):
+        half = n >> (s + 1)
+        if s == 0:
+            source = part.at[j, pl.ds((1 - bits[0]) * half, half)]
+        else:
+            source = give[s - 1].at[j]
+        return pltpu.make_async_remote_copy(
+            src_ref=source,
+            dst_ref=recv[s].at[j],
+            send_sem=send_sem.at[s, j],
+            recv_sem=recv_sem.at[s, j],
+            device_id={"inst": partners[s]},
+            device_id_type=pl.DeviceIdType.MESH,
+        )
+
+    def finish(s, j):
+        copy(s, j).wait_recv()
+        half = n >> (s + 1)
+
+        def total(h):
+            mine = part[j, bits[0] * half + h].astype(jnp.float32) if s == 0 else keep[s - 1][j, h]
+            return mine + recv[s][j, h].astype(jnp.float32)
+
+        if s == stages - 1:
+            out_ref[:, pl.ds(pl.multiple_of(j * chunk, chunk), chunk)] = total(0)
+            return
+        quarter = half // 2
+        for h in range(quarter):
+            give[s][j, h] = total((1 - bits[s + 1]) * quarter + h).astype(jnp.bfloat16)
+        copy(s + 1, j).start()
+        for h in range(quarter):
+            keep[s][j, h] = total(bits[s + 1] * quarter + h)
+
     options = expand_ref.shape[0]
     f32 = jnp.float32
-
-    @pl.when(pl.program_id(0) == 0)
-    def _():
-        held[...] = (pos_ref[...].astype(f32) * contract_size).astype(jnp.bfloat16)
 
     loads = loads_ref[...]
     dims = (((1,), (1,)), ((), ()))
@@ -119,7 +164,27 @@
         return carry
 
     lax.fori_loop(0, options // tile, step, 0)
-    out_ref[...] = jnp.dot(held[...], pnl[...], preferred_element_type=f32).astype(out_ref.dtype)
+    for block in range(n):
+        place = sum(((block >> s) & 1) << (stages - 1 - s) for s in range(stages))
+        part[piece, place] = jnp.dot(
+            pos_ref[block * rows_out : (block + 1) * rows_out, :],
+            pnl[...],
+            preferred_element_type=f32,
+        ).astype(jnp.bfloat16)
+    copy(0, piece).start()
+    for s in range(stages):
+        @pl.when(piece > s)
+        def _():
+            finish(s, piece - 1 - s)
+
+    @pl.when(piece == pieces - 1)
+    def _():
+        for s in range(stages):
+            for j in range(max(0, pieces - 1 - s), pieces):
+                finish(s, j)
+        for s in range(stages):
+            for j in range(pieces):
+                copy(s, j).wait_send()
 
 
 def body(
@@ -172,25 +237,45 @@
     zero = jnp.zeros_like(v0)
     params = jnp.stack([log_k, c1, c2, half_k, half_phi, v0, flat, zero], axis=1)
     chunk = min(256, scen_cols)
+    pieces = scen_cols // chunk
+    stages = n_inst.bit_length() - 1
+    rows = accounts // n_inst
+    held = (contract_size * positions.astype(f32)).astype(jnp.bfloat16)
     whole = pl.BlockSpec(memory_space=pltpu.VMEM)
-    partial = pl.pallas_call(
-        price_kernel,
-        grid=(scen_cols // chunk,),
-        out_shape=jax.ShapeDtypeStruct((accounts, scen_cols), jnp.bfloat16),
+    sizes = [(pieces, n_inst >> (s + 1), rows, chunk) for s in range(stages)]
+    losses = pl.pallas_call(
+        functools.partial(price_kernel, n_inst, stages, pieces),
+        grid=(pieces,),
+        out_shape=jax.ShapeDtypeStruct((rows, scen_cols), f32),
         in_specs=[pl.BlockSpec((chunk, F), lambda i: (i, 0)), whole, whole, whole, whole, whole],
-        out_specs=pl.BlockSpec((accounts, chunk), lambda i: (0, i)),
+        out_specs=whole,
         scratch_shapes=[
-            pltpu.VMEM((accounts, option_rows), jnp.bfloat16),
             pltpu.VMEM((option_rows, chunk), jnp.bfloat16),
             pltpu.VMEM((3 * places, chunk), jnp.bfloat16),
             pltpu.VMEM((3 * places, chunk), jnp.bfloat16),
             pltpu.VMEM((places, chunk), jnp.bfloat16),
             pltpu.VMEM((places, chunk), jnp.bfloat16),
-        ],
-        compiler_params=pltpu.CompilerParams(vmem_limit_bytes=40 * 1024 * 1024),
-    )(factor_returns, loads, base, expand, params, positions)
-    losses = lax.psum_scatter(partial, "inst", scatter_dimension=0, tiled=True).astype(f32)
-    margin = lax.pmax(jnp.max(losses, axis=1), "scen")
+            pltpu.VMEM((pieces, n_inst, rows, chunk), jnp.bfloat16),
+            pltpu.SemaphoreType.DMA((stages, pieces)),
+            pltpu.SemaphoreType.DMA((stages, pieces)),
+        ]
+        + [pltpu.VMEM(size, jnp.bfloat16) for size in sizes]
+        + [pltpu.VMEM(size, jnp.bfloat16) for size in sizes[1:]]
+        + [pltpu.VMEM(size, f32) for size in sizes[1:]],
+        compiler_params=pltpu.CompilerParams(
+            vmem_limit_bytes=40 * 1024 * 1024, collective_id=0, has_side_effects=True
+        ),
+        cost_estimate=pl.CostEstimate(
+            flops=60 * option_rows * scen_cols * 64, bytes_accessed=8 << 20, transcendentals=0
+        ),
+    )(factor_returns, loads, base, expand, params, held)
+    margin = jnp.max(losses, axis=1)
+    n_scen = lax.axis_size("scen")
+    bit = 1
+    while bit < n_scen:
+        pairs = [(i, i ^ bit) for i in range(n_scen)]
+        margin = jnp.maximum(margin, lax.ppermute(margin, "scen", pairs))
+        bit *= 2
     return (losses, margin)
 
 

time: 116 us -> 79 us (0.68)
  waiting for transfers between devices: 48.1 us -> 6.31 us
  Pallas kernels: 21.3 us -> 44.9 us
  blocking collectives: 14 us -> 0 us
  between operations: 14.3 us -> 0.9 us
  local copies, waits for them, and re-layouts: 4.6 us -> 7.87 us
  starting transfers between devices: 6.32 us -> 9.4 us
  other arithmetic: 5.17 us -> 7.15 us
    reduce_scatter x1 -> x0, waiting for transfers between devices: 42.7 us -> none  [body(): lax.psum_scatter(partial, 'inst', scatter_dimension=0, tiled=True)]
    pallas_call x1, Pallas kernels: 21.3 us -> 44.9 us  [body(): pl.pallas_call(functools.partial(price_kernel, n_inst, stages, pieces), g...]
    pmax x1 -> x0, blocking collectives: 14 us -> none  [body(): margin = lax.pmax(jnp.max(losses, axis=1), 'scen')]
    ppermute x0 -> x3, waiting for transfers between devices: none -> 5.25 us  [body(): margin = jnp.maximum(margin, lax.ppermute(margin, 'scen', pairs))]
    all_to_all x1, waiting for transfers between devices: 5.38 us -> 1.06 us  [body(): lax.all_to_all(send.reshape(n_inst, CAP, 256), 'inst', split_axis=0, conc...]
    ppermute x0 -> x3, starting transfers between devices: none -> 3.08 us  [body(): margin = jnp.maximum(margin, lax.ppermute(margin, 'scen', pairs))]
    convert_element_type x0 -> x1, other arithmetic: none -> 2.84 us  [body(): held = (contract_size * positions.astype(f32)).astype(jnp.bfloat16)]
    unnamed x15 -> x20, local copies, waits for them, and re-layouts: 2.41 us -> 4.88 us
  transfers between devices with their start and end apart: 2 -> 4, of which waited for: 2 -> 4; matrix products, arithmetic and copies ran while one was open for 0% -> 6% of each run, Pallas kernels for 0% -> 0%
where the time goes in v4:
time: 79 us; the launch traced here: 78.5 us
  Pallas kernels  44.9 us (57%)
  starting transfers between devices  9.4 us (12%)
  local copies, waits for them, and re-layouts  7.87 us (10%)
  other arithmetic  7.15 us (9%)
  waiting for transfers between devices  6.31 us (8%)
  matrix products  1.95 us (2%)
  between operations  0.9 us (1%)
    pallas_call x1, Pallas kernels, body(): pl.pallas_call(functools.partial(price_kernel, n_inst, stages, pieces), g...  44.9 us
    all_to_all x1, starting transfers between devices, body(): lax.all_to_all(send.reshape(n_inst, CAP, 256), 'inst', split_axis=0, conc...  6.32 us
    ppermute x3, waiting for transfers between devices, body(): margin = jnp.maximum(margin, lax.ppermute(margin, 'scen', pairs))  5.25 us
    unnamed x20, local copies, waits for them, and re-layouts  4.88 us
    ppermute x3, starting transfers between devices, body(): margin = jnp.maximum(margin, lax.ppermute(margin, 'scen', pairs))  3.08 us
    convert_element_type x1, other arithmetic, body(): held = (contract_size * positions.astype(f32)).astype(jnp.bfloat16)  2.84 us
  transfers between devices with their start and end apart: 4, of which 4 were waited for; matrix products, arithmetic and copies ran while one was open for 6% of the time, Pallas kernels for 0%

profile of v4, /device:TPU:0, one launch (start us, length us, event | category | flops | bytes accessed | tf_op | source)
XLA Modules:
  0.0 78.5 jit_solution(8115250944650034016)
XLA Ops:
  0.6 0.0 copy-start
  0.6 0.8 add_select_fusion.5
  1.4 0.7 reshape.99
  2.2 0.7 fusion.19
  2.9 0.7 fusion.6
  3.7 0.0 copy-start.7
  3.7 0.4 fusion.1
  4.2 0.1 slice_compare_fusion
  4.2 0.1 fusion.38
  4.3 0.1 fusion.13
  4.5 0.2 slice_reduce_fusion
  4.7 0.1 select_reduce_fusion.1
  4.8 0.1 convert_add_fusion
  5.0 0.3 select_reduce_fusion
  5.3 0.1 sub.58
  5.4 0.0 copy-done
  5.4 0.4 convolution_convert_fusion
  5.8 0.0 copy-done.7
  5.8 0.3 convolution_convert_fusion.1
  6.1 0.7 copy.32
  6.8 6.3 %all-to-all-start = ((bf16[4,48,256]{2,1,0:T(8,128)(2,1)}), bf16[4,48,256]{2,1,0:T(8,128)(2,1)S(1)}, u32[]{:S(2)}, u32[]{:S(2)}) async-start(bf16[4,48,256]{2,1,0:T(8,128)(2,1)} %bitcast.6), calls=%async_computation | async-start | bytes 196608 | tf_op jit(solution)/shard_map/all_to_all | solution.py:211
  13.2 0.0 copy-start.4
  13.2 0.0 copy-start.5
  13.2 0.0 copy-start.6
  13.2 2.8 %multiply_convert_fusion.pos_ref = bf16[1024,1024]{1,0:T(8,128)(2,1)S(1)} fusion(s32[1024,1024]{1,0:T(8,128)} %param.15), kind=kLoop, calls=%fused_computation | loop fusion | flops 3145728 | bytes 6291456 | tf_op jit(solution)/shard_map/convert_element_type | solution.py:243
  16.1 0.0 copy-done.4
  16.1 0.8 %copy.33.fr_ref = bf16[1024,64]{1,0:T(8,128)(2,1)} copy(bf16[1024,64]{0,1:T(8,128)(2,1)S(1)} %copy-done.4) | data formatting | bytes 262144 | tf_op args[0]
  16.9 1.0 %fusion.3.expand_ref = bf16[1024,192]{1,0:T(8,128)(2,1)} fusion(s32[1024]{0:T(1024)S(1)} %multiply_add_fusion.1), kind=kLoop, calls=%fused_computation.10 | loop fusion | flops 393216 | bytes 397312 | tf_op jit(solution)/shard_map/convert_element_type | solution.py:218
  17.9 1.1 %all-to-all-done = bf16[4,48,256]{2,1,0:T(8,128)(2,1)S(1)} async-done(((bf16[4,48,256]{2,1,0:T(8,128)(2,1)}), bf16[4,48,256]{2,1,0:T(8,128)(2,1)S(1)}, u32[]{:S(2)}, u32[]{:S(2)}) %all-to-all-start) | async-done | bytes 98336 | tf_op jit(solution)/shard_map/all_to_all | solution.py:211
  19.0 0.4 fusion.2
  19.4 0.0 copy-done.5
  19.4 0.0 copy-done.6
  19.5 0.1 stack.31
  19.5 1.0 %copy.34.params_ref = f32[1024,8]{1,0:T(8,128)} copy(f32[1024,8]{0,1:T(8,128)S(1)} %stack.31) | data formatting | bytes 65536 | tf_op jit(solution)/shard_map/stack | solution.py:238
  20.5 1.0 %copy-done.1 = bf16[1024,192]{1,0:T(8,128)(2,1)S(1)} copy-done((bf16[1024,192]{1,0:T(8,128)(2,1)S(1)}, bf16[1024,192]{1,0:T(8,128)(2,1)}, u32[]{:S(2)}) %copy-start.1) | copy-done | bytes 393240
  21.6 0.0 copy-start.2
  21.6 1.0 %copy-done.2 = f32[1024,8]{1,0:T(8,128)S(1)} copy-done((f32[1024,8]{1,0:T(8,128)S(1)}, f32[1024,8]{1,0:T(8,128)}, u32[]{:S(2)}) %copy-start.2) | copy-done | bytes 32792
  22.6 0.9 %copy-done.3 = bf16[1024,64]{1,0:T(8,128)(2,1)S(1)} copy-done((bf16[1024,64]{1,0:T(8,128)(2,1)S(1)}, bf16[1024,64]{1,0:T(8,128)(2,1)}, u32[]{:S(2)}) %copy-start.3) | copy-done | bytes 131096
  23.6 44.9 %shard_map.95 = f32[256,1024]{1,0:T(8,128)S(1)} custom-call(bf16[1024,64]{1,0:T(8,128)(2,1)S(1)} %copy-done.3, bf16[192,128]{1,0:T(8,128)(2,1)S(1)} %slice.41.loads_ref, bf16[192,2]{1,0:T(8,128)(2,1)S(1)} %slice.42.base_ref, bf16[1024,192]{1,0:T(8,128)(2,1)S(1)} %copy-done.1, f32[1024,8]{1,0:T(8,128)S(1)} %copy-done.2, ...), custom_call_target="tpu_custom_call" | custom-call | flops 4026531840 | bytes 8388608 | tf_op jit(solution)/shard_map/pallas_call | solution.py:246
  68.5 0.1 reduce_max.9
  68.6 0.1 collective-permute-start
  68.7 1.1 %collective-permute-done = f32[256]{0:T(256)S(1)} collective-permute-done((f32[256]{0:T(256)S(1)}, f32[256]{0:T(256)S(1)}, u32[]{:S(2)}, u32[]{:S(2)}) %collective-permute-start) | collective-permute-done | bytes 1056 | tf_op jit(solution)/shard_map/ppermute | solution.py:277
  69.8 1.5 %collective-permute-start.1 = (f32[256]{0:T(256)S(1)}, f32[256]{0:T(256)S(1)}, u32[]{:S(2)}, u32[]{:S(2)}) collective-permute-start(f32[256]{0:T(256)S(1)} %max.9), channel_id=1, source_target_pairs={{0,2},{1,3},{2,0},{3,1},{4,6},{5,7},{6,4},{7,5},{8,10},{9,11},{10,... | collective-permute-start | bytes 3080 | tf_op jit(solution)/shard_map/ppermute | solution.py:277
  71.3 2.1 %collective-permute-done.1 = f32[256]{0:T(256)S(1)} collective-permute-done((f32[256]{0:T(256)S(1)}, f32[256]{0:T(256)S(1)}, u32[]{:S(2)}, u32[]{:S(2)}) %collective-permute-start.1) | collective-permute-done | bytes 1056 | tf_op jit(solution)/shard_map/ppermute | solution.py:277
  73.4 1.5 %collective-permute-start.2 = (f32[256]{0:T(256)S(1)}, f32[256]{0:T(256)S(1)}, u32[]{:S(2)}, u32[]{:S(2)}) collective-permute-start(f32[256]{0:T(256)S(1)} %max.10), channel_id=1, source_target_pairs={{0,4},{1,5},{2,6},{3,7},{4,0},{5,1},{6,2},{7,3},{8,12},{9,13},{10,... | collective-permute-start | bytes 3080 | tf_op jit(solution)/shard_map/ppermute | solution.py:277
  74.9 2.0 %collective-permute-done.2 = f32[256]{0:T(256)S(1)} collective-permute-done((f32[256]{0:T(256)S(1)}, f32[256]{0:T(256)S(1)}, u32[]{:S(2)}, u32[]{:S(2)}) %collective-permute-start.2) | collective-permute-done | bytes 1056 | tf_op jit(solution)/shard_map/ppermute | solution.py:277
  76.9 0.6 max.11
  77.5 1.0 %copy.44 = f32[256,1024]{1,0:T(8,128)} copy(f32[256,1024]{1,0:T(8,128)S(1)} %shard_map.95) | data formatting | bytes 2097152
  (26 shorter events, 0.3 us)
Async XLA Ops:
  0.6 4.7 %copy-start = (bf16[1000,128]{1,0:T(8,128)(2,1)S(1)}, bf16[1000,128]{1,0:T(8,128)(2,1)}, u32[]{:S(2)}) copy-start(bf16[1000,128]{1,0:T(8,128)(2,1)} %param.9) | copy-start | bytes 768004
  3.7 2.1 %copy-start.7 = (bf16[2,1000]{1,0:T(2,128)(2,1)S(1)}, bf16[2,1000]{1,0:T(2,128)(2,1)}, u32[]{:S(2)}) copy-start(bf16[2,1000]{1,0:T(2,128)(2,1)} %param.10) | copy-start | bytes 12004
  6.8 12.2 %all-to-all-start = ((bf16[4,48,256]{2,1,0:T(8,128)(2,1)}), bf16[4,48,256]{2,1,0:T(8,128)(2,1)S(1)}, u32[]{:S(2)}, u32[]{:S(2)}) async-start(bf16[4,48,256]{2,1,0:T(8,128)(2,1)} %bitcast.6), calls=%async_computation | async-start | bytes 196608 | tf_op jit(solution)/shard_map/all_to_all | solution.py:211
  13.2 2.9 %copy-start.4 = (bf16[1024,64]{0,1:T(8,128)(2,1)S(1)}, bf16[1024,64]{0,1:T(8,128)(2,1)}, u32[]{:S(2)}) copy-start(bf16[1024,64]{0,1:T(8,128)(2,1)} %param.8) | copy-start | bytes 393220
  13.2 6.2 %copy-start.5 = (s32[1024]{0:T(1024)S(1)}, s32[1024]{0:T(1024)}, u32[]{:S(2)}) copy-start(s32[1024]{0:T(1024)} %param.13) | copy-start | bytes 12292
  13.2 6.2 %copy-start.6 = (f32[1024]{0:T(1024)S(1)}, f32[1024]{0:T(1024)}, u32[]{:S(2)}) copy-start(f32[1024]{0:T(1024)} %param.14) | copy-start | bytes 12292
  20.5 1.0 %copy-start.1 = (bf16[1024,192]{1,0:T(8,128)(2,1)S(1)}, bf16[1024,192]{1,0:T(8,128)(2,1)}, u32[]{:S(2)}) copy-start(bf16[1024,192]{1,0:T(8,128)(2,1)} %fusion.3.expand_ref) | copy-start | bytes 1179652
  21.6 1.0 %copy-start.2 = (f32[1024,8]{1,0:T(8,128)S(1)}, f32[1024,8]{1,0:T(8,128)}, u32[]{:S(2)}) copy-start(f32[1024,8]{1,0:T(8,128)} %copy.34.params_ref) | copy-start | bytes 98308
  22.6 0.9 %copy-start.3 = (bf16[1024,64]{1,0:T(8,128)(2,1)S(1)}, bf16[1024,64]{1,0:T(8,128)(2,1)}, u32[]{:S(2)}) copy-start(bf16[1024,64]{1,0:T(8,128)(2,1)} %copy.33.fr_ref) | copy-start | bytes 393220
  68.6 1.2 %collective-permute-start = (f32[256]{0:T(256)S(1)}, f32[256]{0:T(256)S(1)}, u32[]{:S(2)}, u32[]{:S(2)}) collective-permute-start(f32[256]{0:T(256)S(1)} %reduce_max.9), channel_id=1, source_target_pairs={{0,1},{1,0},{2,3},{3,2},{4,5},{5,4},{6,7},{7,6},{8,9},{9,8},{10,11... | collective-permute-start | bytes 3080 | tf_op jit(solution)/shard_map/ppermute | solution.py:277
  69.8 3.6 %collective-permute-start.1 = (f32[256]{0:T(256)S(1)}, f32[256]{0:T(256)S(1)}, u32[]{:S(2)}, u32[]{:S(2)}) collective-permute-start(f32[256]{0:T(256)S(1)} %max.9), channel_id=1, source_target_pairs={{0,2},{1,3},{2,0},{3,1},{4,6},{5,7},{6,4},{7,5},{8,10},{9,11},{10,... | collective-permute-start | bytes 3080 | tf_op jit(solution)/shard_map/ppermute | solution.py:277
  73.4 3.6 %collective-permute-start.2 = (f32[256]{0:T(256)S(1)}, f32[256]{0:T(256)S(1)}, u32[]{:S(2)}, u32[]{:S(2)}) collective-permute-start(f32[256]{0:T(256)S(1)} %max.10), channel_id=1, source_target_pairs={{0,4},{1,5},{2,6},{3,7},{4,0},{5,1},{6,2},{7,3},{8,12},{9,13},{10,... | collective-permute-start | bytes 3080 | tf_op jit(solution)/shard_map/ppermute | solution.py:277

commit v5 on v4

--- a/solution.py
+++ b/solution.py
@@ -73,12 +73,58 @@
     return send_row, my_owner * CAP + rank_here
 
 
-def price_kernel(n, stages, pieces, fr_ref, loads_ref, base_ref, expand_ref, params_ref, pos_ref, out_ref, pnl, lf_sc, rv_sc, f_sc, v_sc, part, send_sem, recv_sem, *buffers):
+def swap_kernel(n, send_ref, pos_ref, got_ref, held_ref, landing, send_sem, recv_sem):
+    me = lax.axis_index("inst")
+    barrier = pltpu.get_barrier_semaphore()
+    for d in range(1, n):
+        pl.semaphore_signal(
+            barrier,
+            inc=1,
+            device_id={"inst": (me + d) % n},
+            device_id_type=pl.DeviceIdType.MESH,
+        )
+    pl.semaphore_wait(barrier, n - 1)
+    copies = []
+    for d in range(1, n):
+        copies.append(
+            pltpu.make_async_remote_copy(
+                src_ref=send_ref.at[(me + d) % n],
+                dst_ref=landing.at[d - 1],
+                send_sem=send_sem.at[d - 1],
+                recv_sem=recv_sem.at[d - 1],
+                device_id={"inst": (me + d) % n},
+                device_id_type=pl.DeviceIdType.MESH,
+            )
+        )
+    for one in copies:
+        one.start()
+    got_ref[me] = send_ref[me]
+    tile = 64
+
+    def step(index, carry):
+        rows = pl.ds(pl.multiple_of(index * tile, tile), tile)
+        wide = pos_ref[rows, :].astype(jnp.float32) * contract_size
+        held_ref[rows, :] = wide.astype(jnp.bfloat16)
+        return carry
+
+    lax.fori_loop(0, pos_ref.shape[0] // tile, step, 0)
+    for d, one in enumerate(copies, 1):
+        one.wait_recv()
+        got_ref[(me + n - d) % n] = landing[d - 1]
+    for one in copies:
+        one.wait_send()
+
+
+def price_kernel(n, stages, pieces, scen_stages, fr_ref, loads_ref, base_ref, expand_ref, params_ref, pos_ref, out_ref, top_ref, pnl, lf_sc, rv_sc, f_sc, v_sc, part, send_sem, recv_sem, best, beside, top_send, top_recv, *buffers):
     recv, give, keep = buffers[:stages], buffers[stages : 2 * stages - 1], buffers[2 * stages - 1 :]
     piece = pl.program_id(0)
     me = lax.axis_index("inst")
     bits = [(me // (1 << s)) % 2 for s in range(stages)]
     partners = [me + (1 << s) * (1 - 2 * bits[s]) for s in range(stages)]
+    place_scen = lax.axis_index("scen")
+    mates = [
+        place_scen + (1 << s) * (1 - 2 * ((place_scen // (1 << s)) % 2)) for s in range(scen_stages)
+    ]
     rows_out, chunk = out_ref.shape[0], fr_ref.shape[0]
 
     @pl.when(piece == 0)
@@ -88,7 +134,11 @@
             pl.semaphore_signal(
                 barrier, inc=1, device_id={"inst": partner}, device_id_type=pl.DeviceIdType.MESH
             )
-        pl.semaphore_wait(barrier, stages)
+        for mate in mates:
+            pl.semaphore_signal(
+                barrier, inc=1, device_id={"scen": mate}, device_id_type=pl.DeviceIdType.MESH
+            )
+        pl.semaphore_wait(barrier, stages + scen_stages)
 
     def copy(s, j):
         half = n >> (s + 1)
@@ -182,6 +232,28 @@
         for s in range(stages):
             for j in range(max(0, pieces - 1 - s), pieces):
                 finish(s, j)
+        top = out_ref[:, 0:128]
+        for at in range(128, out_ref.shape[1], 128):
+            top = jnp.maximum(top, out_ref[:, at : at + 128])
+        top = jnp.max(top.T, axis=0, keepdims=True)
+        best[0] = jnp.broadcast_to(top, best.shape[1:])
+        hops = []
+        for s in range(scen_stages):
+            hop = pltpu.make_async_remote_copy(
+                src_ref=best.at[s],
+                dst_ref=beside.at[s],
+                send_sem=top_send.at[s],
+                recv_sem=top_recv.at[s],
+                device_id={"scen": mates[s]},
+                device_id_type=pl.DeviceIdType.MESH,
+            )
+            hop.start()
+            hop.wait_recv()
+            best[s + 1] = jnp.maximum(best[s], beside[s])
+            hops.append(hop)
+        top_ref[...] = best[scen_stages]
+        for hop in hops:
+            hop.wait_send()
         for s in range(stages):
             for j in range(pieces):
                 copy(s, j).wait_send()
@@ -208,9 +280,25 @@
         select, base_state, (((1,), (1,)), ((), ())), preferred_element_type=f32
     ).astype(jnp.bfloat16)
     send = jnp.concatenate([send_loads, jnp.pad(send_base, ((0, 0), (0, 126)))], axis=1)
-    got = lax.all_to_all(
-        send.reshape(n_inst, CAP, 256), "inst", split_axis=0, concat_axis=0, tiled=True
-    ).reshape(n_inst * CAP, 256)
+    whole = pl.BlockSpec(memory_space=pltpu.VMEM)
+    got, held = pl.pallas_call(
+        functools.partial(swap_kernel, n_inst),
+        out_shape=(
+            jax.ShapeDtypeStruct((n_inst, CAP, 256), jnp.bfloat16),
+            jax.ShapeDtypeStruct((accounts, option_rows), jnp.bfloat16),
+        ),
+        in_specs=[whole, whole],
+        out_specs=(whole, whole),
+        scratch_shapes=[
+            pltpu.VMEM((n_inst - 1, CAP, 256), jnp.bfloat16),
+            pltpu.SemaphoreType.DMA((n_inst - 1,)),
+            pltpu.SemaphoreType.DMA((n_inst - 1,)),
+        ],
+        compiler_params=pltpu.CompilerParams(
+            vmem_limit_bytes=16 * 1024 * 1024, collective_id=1, has_side_effects=True
+        ),
+    )(send.reshape(n_inst, CAP, 256), positions)
+    got = got.reshape(n_inst * CAP, 256)
     loads = got[:, :128]
     base = got[:, 128:130]
     places = n_inst * CAP
@@ -240,15 +328,17 @@
     pieces = scen_cols // chunk
     stages = n_inst.bit_length() - 1
     rows = accounts // n_inst
-    held = (contract_size * positions.astype(f32)).astype(jnp.bfloat16)
-    whole = pl.BlockSpec(memory_space=pltpu.VMEM)
+    scen_stages = lax.axis_size("scen").bit_length() - 1
     sizes = [(pieces, n_inst >> (s + 1), rows, chunk) for s in range(stages)]
-    losses = pl.pallas_call(
-        functools.partial(price_kernel, n_inst, stages, pieces),
+    losses, top = pl.pallas_call(
+        functools.partial(price_kernel, n_inst, stages, pieces, scen_stages),
         grid=(pieces,),
-        out_shape=jax.ShapeDtypeStruct((rows, scen_cols), f32),
+        out_shape=(
+            jax.ShapeDtypeStruct((rows, scen_cols), f32),
+            jax.ShapeDtypeStruct((8, rows), f32),
+        ),
         in_specs=[pl.BlockSpec((chunk, F), lambda i: (i, 0)), whole, whole, whole, whole, whole],
-        out_specs=whole,
+        out_specs=(whole, whole),
         scratch_shapes=[
             pltpu.VMEM((option_rows, chunk), jnp.bfloat16),
             pltpu.VMEM((3 * places, chunk), jnp.bfloat16),
@@ -258,24 +348,22 @@
             pltpu.VMEM((pieces, n_inst, rows, chunk), jnp.bfloat16),
             pltpu.SemaphoreType.DMA((stages, pieces)),
             pltpu.SemaphoreType.DMA((stages, pieces)),
+            pltpu.VMEM((scen_stages + 1, 8, rows), f32),
+            pltpu.VMEM((scen_stages, 8, rows), f32),
+            pltpu.SemaphoreType.DMA((scen_stages,)),
+            pltpu.SemaphoreType.DMA((scen_stages,)),
         ]
         + [pltpu.VMEM(size, jnp.bfloat16) for size in sizes]
         + [pltpu.VMEM(size, jnp.bfloat16) for size in sizes[1:]]
         + [pltpu.VMEM(size, f32) for size in sizes[1:]],
         compiler_params=pltpu.CompilerParams(
-            vmem_limit_bytes=40 * 1024 * 1024, collective_id=0, has_side_effects=True
+            vmem_limit_bytes=24 * 1024 * 1024, collective_id=0, has_side_effects=True
         ),
         cost_estimate=pl.CostEstimate(
             flops=60 * option_rows * scen_cols * 64, bytes_accessed=8 << 20, transcendentals=0
         ),
     )(factor_returns, loads, base, expand, params, held)
-    margin = jnp.max(losses, axis=1)
-    n_scen = lax.axis_size("scen")
-    bit = 1
-    while bit < n_scen:
-        pairs = [(i, i ^ bit) for i in range(n_scen)]
-        margin = jnp.maximum(margin, lax.ppermute(margin, "scen", pairs))
-        bit *= 2
+    margin = top[0]
     return (losses, margin)
 
 

time: 79 us -> 76.7 us (0.971)
  Pallas kernels: 44.9 us -> 61.3 us
  starting transfers between devices: 9.4 us -> 0 us
  waiting for transfers between devices: 6.31 us -> 0 us
  other arithmetic: 7.15 us -> 2.78 us
  local copies, waits for them, and re-layouts: 7.87 us -> 9.34 us
    pallas_call x1 -> x2, Pallas kernels: 44.9 us -> 61.3 us  [the longest x1 53.4 us: body(): pl.pallas_call(functools.partial(price_kernel, n_inst, stages, pieces, sc...]
    all_to_all x1 -> x0, starting transfers between devices: 6.32 us -> none  [body(): lax.all_to_all(send.reshape(n_inst, CAP, 256), 'inst', split_axis=0, conc...]
    ppermute x3 -> x0, waiting for transfers between devices: 5.25 us -> none  [body(): margin = jnp.maximum(margin, lax.ppermute(margin, 'scen', pairs))]
    ppermute x3 -> x0, starting transfers between devices: 3.08 us -> none  [body(): margin = jnp.maximum(margin, lax.ppermute(margin, 'scen', pairs))]
    convert_element_type x1 -> x0, other arithmetic: 2.84 us -> none  [body(): held = (contract_size * positions.astype(f32)).astype(jnp.bfloat16)]
    unnamed x20 -> x18, local copies, waits for them, and re-layouts: 4.88 us -> 7.19 us
    all_to_all x1 -> x0, waiting for transfers between devices: 1.06 us -> none  [body(): lax.all_to_all(send.reshape(n_inst, CAP, 256), 'inst', split_axis=0, conc...]
    another operation x3, local copies, waits for them, and re-layouts: 1.07 us -> 0.26 us  [body(): jnp.stack([log_k, c1, c2, half_k, half_phi, v0, flat, zero], axis=1)]
  transfers between devices with their start and end apart: 4 -> 0, of which waited for: 4 -> 0; matrix products, arithmetic and copies ran while one was open for 6% -> 0% of each run, Pallas kernels for 0% -> 0%
where the time goes in v5:
time: 76.7 us; the launch traced here: 76.3 us
  Pallas kernels  61.3 us (80%)
  local copies, waits for them, and re-layouts  9.34 us (12%)
  other arithmetic  2.78 us (4%)
  matrix products  1.96 us (3%)
  between operations  0.91 us (1%)
    pallas_call x1, Pallas kernels, body(): pl.pallas_call(functools.partial(price_kernel, n_inst, stages, pieces, sc...  53.4 us
    pallas_call x1, Pallas kernels, body(): pl.pallas_call(functools.partial(swap_kernel, n_inst), out_shape=(jax.Sha...  7.89 us
    unnamed x18, local copies, waits for them, and re-layouts  7.19 us

profile of v5, /device:TPU:0, one launch (start us, length us, event | category | flops | bytes accessed | tf_op | source)
XLA Modules:
  0.0 76.3 jit_solution(5457640753523065160)
XLA Ops:
  0.6 0.0 copy-start
  0.7 0.8 %reshape.99 = s32[4,1024]{1,0:T(4,128)S(1)} reshape(s32[4096]{0:T(1024)} %param.12) | data formatting | bytes 32768 | tf_op jit(solution)/shard_map/reshape | solution.py:45
  1.4 0.1 slice_compare_fusion
  1.5 0.1 fusion.38
  1.6 0.7 fusion.19
  2.4 0.7 add_select_fusion.5
  3.1 1.1 %copy.29.fr_ref = bf16[1024,64]{1,0:T(8,128)(2,1)S(1)} copy(bf16[1024,64]{0,1:T(8,128)(2,1)} %param.8) | data formatting | bytes 262144 | tf_op args[0]
  4.2 0.7 fusion.6
  4.9 0.0 copy-start.6
  4.9 0.4 fusion.1
  5.5 0.1 fusion.13
  5.6 0.2 slice_reduce_fusion
  5.8 0.1 select_reduce_fusion.1
  5.9 0.1 convert_add_fusion
  6.2 0.3 select_reduce_fusion
  6.4 0.1 sub.58
  6.5 0.0 copy-done.6
  6.5 0.3 convolution_convert_fusion.1
  6.8 0.0 copy-done
  6.8 0.4 convolution_convert_fusion
  7.2 0.1 copy.28
  7.3 0.2 fusion.3.expand_ref
  7.5 0.0 copy-start.1
  7.6 2.2 %copy-done.1 = s32[1024,1024]{1,0:T(8,128)S(1)} copy-done((s32[1024,1024]{1,0:T(8,128)S(1)}, s32[1024,1024]{1,0:T(8,128)}, u32[]{:S(2)}) %copy-start.1) | copy-done | bytes 4194328
  9.7 0.0 copy-start.4
  9.7 0.0 copy-start.5
  9.7 7.9 %shard_map.95 = (bf16[4,48,256]{2,1,0:T(8,128)(2,1)S(1)}, bf16[1024,1024]{1,0:T(8,128)(2,1)S(1)}) custom-call(bf16[4,48,256]{2,1,0:T(8,128)(2,1)S(1)} %bitcast.66, s32[1024,1024]{1,0:T(8,128)S(1)} %copy-done.1), custom_call_target="tpu_custom_call" | custom-call | tf_op jit(solution)/shard_map/pallas_call | solution.py:284
  17.6 0.0 copy-start.2
  17.6 1.3 %copy-done.2 = bf16[1024,1024]{1,0:T(8,128)(2,1)} copy-done((bf16[1024,1024]{1,0:T(8,128)(2,1)}, bf16[1024,1024]{1,0:T(8,128)(2,1)S(1)}, u32[]{:S(2)}) %copy-start.2) | copy-done | bytes 2097176
  19.0 0.4 fusion.2
  19.4 0.0 copy-done.4
  19.4 0.0 copy-done.5
  19.4 0.1 stack.31
  19.5 0.2 copy.30.params_ref
  19.7 0.0 copy-start.3
  19.7 1.6 %copy-done.3 = bf16[1024,1024]{1,0:T(8,128)(2,1)S(1)} copy-done((bf16[1024,1024]{1,0:T(8,128)(2,1)S(1)}, bf16[1024,1024]{1,0:T(8,128)(2,1)}, u32[]{:S(2)}) %copy-start.3) | copy-done | bytes 2097176
  21.3 53.4 %shard_map.96 = (f32[256,1024]{1,0:T(8,128)S(1)}, f32[8,256]{1,0:T(8,128)S(1)}) custom-call(bf16[1024,64]{1,0:T(8,128)(2,1)S(1)} %copy.29.fr_ref, bf16[192,128]{1,0:T(8,128)(2,1)S(1)} %slice.45.loads_ref, bf16[192,2]{1,0:T(8,128)(2,1)S(1)} %slice.46.base_ref, bf16[1024,192]{1,0:T(8,128)(2,1)S(1)} %fusion.3.expand_ref, f32[1024,8]{1,0:T(8,128)S(1)} %copy.30.params_ref, ...), custom_call_target="tpu_custom_call" | custom-call | flops 4026531840 | bytes 8388608 | tf_op jit(solution)/shard_map/pallas_call | solution.py:333
  74.7 0.6 slice.39
  75.3 1.0 %copy.40 = f32[256,1024]{1,0:T(8,128)} copy(f32[256,1024]{1,0:T(8,128)S(1)} %get-tuple-element.31) | data formatting | bytes 2097152
  (22 shorter events, 0.3 us)
Async XLA Ops:
  0.6 6.2 %copy-start = (bf16[1000,128]{1,0:T(8,128)(2,1)S(1)}, bf16[1000,128]{1,0:T(8,128)(2,1)}, u32[]{:S(2)}) copy-start(bf16[1000,128]{1,0:T(8,128)(2,1)} %param.9) | copy-start | bytes 768004
  4.9 1.6 %copy-start.6 = (bf16[2,1000]{1,0:T(2,128)(2,1)S(1)}, bf16[2,1000]{1,0:T(2,128)(2,1)}, u32[]{:S(2)}) copy-start(bf16[2,1000]{1,0:T(2,128)(2,1)} %param.10) | copy-start | bytes 12004
  7.5 2.2 %copy-start.1 = (s32[1024,1024]{1,0:T(8,128)S(1)}, s32[1024,1024]{1,0:T(8,128)}, u32[]{:S(2)}) copy-start(s32[1024,1024]{1,0:T(8,128)} %pos_ref.1) | copy-start | bytes 12582916
  9.7 9.6 %copy-start.4 = (s32[1024]{0:T(1024)S(1)}, s32[1024]{0:T(1024)}, u32[]{:S(2)}) copy-start(s32[1024]{0:T(1024)} %param.13) | copy-start | bytes 12292
  9.7 9.6 %copy-start.5 = (f32[1024]{0:T(1024)S(1)}, f32[1024]{0:T(1024)}, u32[]{:S(2)}) copy-start(f32[1024]{0:T(1024)} %param.14) | copy-start | bytes 12292
  17.6 1.3 %copy-start.2 = (bf16[1024,1024]{1,0:T(8,128)(2,1)}, bf16[1024,1024]{1,0:T(8,128)(2,1)S(1)}, u32[]{:S(2)}) copy-start(bf16[1024,1024]{1,0:T(8,128)(2,1)S(1)} %get-tuple-element.7.pos_ref) | copy-start | bytes 6291460
  19.7 1.6 %copy-start.3 = (bf16[1024,1024]{1,0:T(8,128)(2,1)S(1)}, bf16[1024,1024]{1,0:T(8,128)(2,1)}, u32[]{:S(2)}) copy-start(bf16[1024,1024]{1,0:T(8,128)(2,1)} %copy-done.2) | copy-start | bytes 6291460

commit v6 on v5

--- a/solution.py
+++ b/solution.py
@@ -324,7 +324,7 @@
     flat = v0 + half_phi * strike
     zero = jnp.zeros_like(v0)
     params = jnp.stack([log_k, c1, c2, half_k, half_phi, v0, flat, zero], axis=1)
-    chunk = min(256, scen_cols)
+    chunk = min(128, scen_cols)
     pieces = scen_cols // chunk
     stages = n_inst.bit_length() - 1
     rows = accounts // n_inst

time: 76.7 us -> 78 us (1.017)
  Pallas kernels: 61.3 us -> 62.5 us
    pallas_call x1, Pallas kernels: 53.4 us -> 54.7 us  [body(): pl.pallas_call(functools.partial(price_kernel, n_inst, stages, pieces, sc...]
where the time goes in v6:
time: 78 us; the launch traced here: 77.5 us
  Pallas kernels  62.5 us (80%)
  local copies, waits for them, and re-layouts  9.34 us (12%)
  other arithmetic  2.78 us (4%)
  matrix products  1.96 us (3%)
  between operations  0.91 us (1%)
    pallas_call x1, Pallas kernels, body(): pl.pallas_call(functools.partial(price_kernel, n_inst, stages, pieces, sc...  54.7 us
    pallas_call x1, Pallas kernels, body(): pl.pallas_call(functools.partial(swap_kernel, n_inst), out_shape=(jax.Sha...  7.89 us
    unnamed x18, local copies, waits for them, and re-layouts  7.19 us

profile of v6, /device:TPU:0, one launch (start us, length us, event | category | flops | bytes accessed | tf_op | source)
XLA Modules:
  0.0 77.5 jit_solution(15937338356110816371)
XLA Ops:
  0.6 0.0 copy-start
  0.7 0.8 reshape.99
  1.4 0.1 slice_compare_fusion
  1.5 0.1 fusion.38
  1.6 0.7 fusion.19
  2.4 0.7 add_select_fusion.5
  3.1 1.1 %copy.29.fr_ref = bf16[1024,64]{1,0:T(8,128)(2,1)S(1)} copy(bf16[1024,64]{0,1:T(8,128)(2,1)} %param.8) | data formatting | bytes 262144 | tf_op args[0]
  4.2 0.7 fusion.6
  4.9 0.0 copy-start.6
  4.9 0.4 fusion.1
  5.5 0.1 fusion.13
  5.6 0.2 slice_reduce_fusion
  5.8 0.1 select_reduce_fusion.1
  5.9 0.1 convert_add_fusion
  6.2 0.3 select_reduce_fusion
  6.4 0.1 sub.58
  6.5 0.0 copy-done.6
  6.5 0.3 convolution_convert_fusion.1
  6.8 0.0 copy-done
  6.8 0.4 convolution_convert_fusion
  7.2 0.1 copy.28
  7.3 0.2 fusion.3.expand_ref
  7.5 0.0 copy-start.1
  7.6 2.2 %copy-done.1 = s32[1024,1024]{1,0:T(8,128)S(1)} copy-done((s32[1024,1024]{1,0:T(8,128)S(1)}, s32[1024,1024]{1,0:T(8,128)}, u32[]{:S(2)}) %copy-start.1) | copy-done | bytes 4194328
  9.7 0.0 copy-start.4
  9.7 0.0 copy-start.5
  9.7 7.9 %shard_map.95 = (bf16[4,48,256]{2,1,0:T(8,128)(2,1)S(1)}, bf16[1024,1024]{1,0:T(8,128)(2,1)S(1)}) custom-call(bf16[4,48,256]{2,1,0:T(8,128)(2,1)S(1)} %bitcast.66, s32[1024,1024]{1,0:T(8,128)S(1)} %copy-done.1), custom_call_target="tpu_custom_call" | custom-call | tf_op jit(solution)/shard_map/pallas_call | solution.py:284
  17.6 0.0 copy-start.2
  17.6 1.3 %copy-done.2 = bf16[1024,1024]{1,0:T(8,128)(2,1)} copy-done((bf16[1024,1024]{1,0:T(8,128)(2,1)}, bf16[1024,1024]{1,0:T(8,128)(2,1)S(1)}, u32[]{:S(2)}) %copy-start.2) | copy-done | bytes 2097176
  19.0 0.4 fusion.2
  19.4 0.0 copy-done.4
  19.4 0.0 copy-done.5
  19.4 0.1 stack.31
  19.5 0.2 copy.30.params_ref
  19.7 0.0 copy-start.3
  19.7 1.6 %copy-done.3 = bf16[1024,1024]{1,0:T(8,128)(2,1)S(1)} copy-done((bf16[1024,1024]{1,0:T(8,128)(2,1)S(1)}, bf16[1024,1024]{1,0:T(8,128)(2,1)}, u32[]{:S(2)}) %copy-start.3) | copy-done | bytes 2097176
  21.3 54.7 %shard_map.96 = (f32[256,1024]{1,0:T(8,128)S(1)}, f32[8,256]{1,0:T(8,128)S(1)}) custom-call(bf16[1024,64]{1,0:T(8,128)(2,1)S(1)} %copy.29.fr_ref, bf16[192,128]{1,0:T(8,128)(2,1)S(1)} %slice.45.loads_ref, bf16[192,2]{1,0:T(8,128)(2,1)S(1)} %slice.46.base_ref, bf16[1024,192]{1,0:T(8,128)(2,1)S(1)} %fusion.3.expand_ref, f32[1024,8]{1,0:T(8,128)S(1)} %copy.30.params_ref, ...), custom_call_target="tpu_custom_call" | custom-call | flops 4026531840 | bytes 8388608 | tf_op jit(solution)/shard_map/pallas_call | solution.py:333
  76.0 0.6 slice.39
  76.6 1.0 %copy.40 = f32[256,1024]{1,0:T(8,128)} copy(f32[256,1024]{1,0:T(8,128)S(1)} %get-tuple-element.31) | data formatting | bytes 2097152
  (22 shorter events, 0.3 us)
Async XLA Ops:
  0.6 6.2 %copy-start = (bf16[1000,128]{1,0:T(8,128)(2,1)S(1)}, bf16[1000,128]{1,0:T(8,128)(2,1)}, u32[]{:S(2)}) copy-start(bf16[1000,128]{1,0:T(8,128)(2,1)} %param.9) | copy-start | bytes 768004
  4.9 1.6 %copy-start.6 = (bf16[2,1000]{1,0:T(2,128)(2,1)S(1)}, bf16[2,1000]{1,0:T(2,128)(2,1)}, u32[]{:S(2)}) copy-start(bf16[2,1000]{1,0:T(2,128)(2,1)} %param.10) | copy-start | bytes 12004
  7.5 2.2 %copy-start.1 = (s32[1024,1024]{1,0:T(8,128)S(1)}, s32[1024,1024]{1,0:T(8,128)}, u32[]{:S(2)}) copy-start(s32[1024,1024]{1,0:T(8,128)} %pos_ref.1) | copy-start | bytes 12582916
  9.7 9.6 %copy-start.4 = (s32[1024]{0:T(1024)S(1)}, s32[1024]{0:T(1024)}, u32[]{:S(2)}) copy-start(s32[1024]{0:T(1024)} %param.13) | copy-start | bytes 12292
  9.7 9.6 %copy-start.5 = (f32[1024]{0:T(1024)S(1)}, f32[1024]{0:T(1024)}, u32[]{:S(2)}) copy-start(f32[1024]{0:T(1024)} %param.14) | copy-start | bytes 12292
  17.6 1.3 %copy-start.2 = (bf16[1024,1024]{1,0:T(8,128)(2,1)}, bf16[1024,1024]{1,0:T(8,128)(2,1)S(1)}, u32[]{:S(2)}) copy-start(bf16[1024,1024]{1,0:T(8,128)(2,1)S(1)} %get-tuple-element.7.pos_ref) | copy-start | bytes 6291460
  19.7 1.6 %copy-start.3 = (bf16[1024,1024]{1,0:T(8,128)(2,1)S(1)}, bf16[1024,1024]{1,0:T(8,128)(2,1)}, u32[]{:S(2)}) copy-start(bf16[1024,1024]{1,0:T(8,128)(2,1)} %copy-done.2) | copy-start | bytes 6291460
